TPU v7x, 128 devices: a whole 4x4x4 slice. The times are simulated.
128 devices in a mesh: row: 16 (over y, x), col: 8 (over z, core).
Axes of the slice: x: 4, y: 4, z: 4, core: 2. Of those that a mesh axis runs over, the one named last changes fastest.
Arguments:
- hamilton: float32 [24576, 24576], P('row', 'col'), as said below
- start_block: float32 [48, 24576], P(None, 'col'), may hold values from -6 to 6
- bounds: float32 [3], replicated, as said below
- degree_pick: int32 [48], replicated, may hold values from 0 to 1
Outputs:
- basis: float32 [48, 24576], P(None, 'col')
Inputs may be any that keep to these rules, and one draw needn't show every extreme that they name: hamilton is symmetric and all its eigenvalues lie between bounds[0] and bounds[2]. bounds[0] < bounds[1] < bounds[2].
All inputs are finite; a program needn't handle non-finite values.
Results may differ from a plain program's by a relative error of at most 0.0003.
Values sent between devices are 32-bit elements; how exact they have to be, the bound alone decides.
A program may use at most 128 MiB of HBM per device.

v0:
```python
import jax
import jax.numpy as jnp
from jax import lax
from jax.sharding import PartitionSpec as P

DLO = 6
DHI = 10


def on_device(hamilton, start_block, bounds, degree_pick):
    rows_dev, cols_dev = hamilton.shape
    vectors = start_block.shape[0]
    row_at = lax.axis_index("row")
    col_at = lax.axis_index("col")
    offset = row_at * rows_dev - col_at * cols_dev
    inside = (offset >= 0) & (offset < cols_dev)
    start_at = jnp.where(inside, offset, 0)
    diag_weight = jnp.where(inside, 1.0, 0.0).astype(jnp.float32)
    lowest = bounds[0]
    lower_end = bounds[1]
    upper_end = bounds[2]
    half_width = (upper_end - lower_end) / 2.0
    center = (upper_end + lower_end) / 2.0
    sigma_one = half_width / (lowest - center)

    def toward_rows(block):
        part_sum = lax.dot_general(
            block, hamilton, (((1,), (1,)), ((), ())), precision=lax.Precision.HIGHEST
        )
        diag_part = lax.dynamic_slice_in_dim(block, start_at, rows_dev, 1)
        return part_sum - center * diag_weight * diag_part

    def toward_cols(block):
        part_sum = jnp.dot(block, hamilton, precision=lax.Precision.HIGHEST)
        placed = lax.dynamic_update_slice_in_dim(
            jnp.zeros((vectors, cols_dev), jnp.float32), block, start_at, 1
        )
        return part_sum - center * diag_weight * placed

    sigma = sigma_one
    previous = jnp.zeros((vectors, rows_dev), jnp.float32)
    current = start_block
    scale = sigma_one / half_width
    coeff = jnp.float32(0.0) * sigma
    kept = start_block
    for step in range(1, DHI + 1):
        if step > 1:
            new_sigma = 1.0 / (2.0 / sigma_one - sigma)
            scale = 2.0 * new_sigma / half_width
            coeff = sigma * new_sigma
            sigma = new_sigma
        odd = step % 2 == 1
        partial_value = toward_rows(current) if odd else toward_cols(current)
        if odd:
            total = lax.psum(partial_value, "col")
        else:
            total = lax.psum(partial_value, "row")
        following = scale * total - coeff * previous
        previous, current = (current, following)
        if step == DLO:
            kept = current
    filtered = jnp.where(degree_pick[:, None] == 0, kept, current)

    def gram_of(block):
        local_gram = jnp.dot(block, block.T, precision=lax.Precision.HIGHEST)
        return lax.psum(local_gram, "col")

    def cholesky_step(block):
        lower_factor = jnp.linalg.cholesky(gram_of(block))
        return lax.linalg.triangular_solve(lower_factor, block, left_side=True, lower=True)

    first = cholesky_step(filtered)
    second = cholesky_step(first)
    order = cols_dev * lax.axis_size("col")
    return second * jnp.sqrt(jnp.float32(order))


def solution(mesh):
    in_specs = (P("row", "col"), P(None, "col"), P(), P())
    out_specs = P(None, "col")
    return jax.shard_map(
        on_device, mesh=mesh, in_specs=in_specs, out_specs=out_specs, check_vma=False
    )
```

profile of v0, /device:TPU:1, one launch (start us, length us, event | category | flops | bytes accessed | tf_op | source)
XLA Modules:
  0.0 1002.2 jit_solution(7641148819625392898)
XLA Ops:
  6.5 1.4 fusion.13
  9.2 22.0 %convolution_subtract_fusion.9 = f32[48,1536]{1,0:T(8,128)} fusion(f32[48,3072]{1,0:T(8,128)} %param.8, f32[1536,3072]{1,0:T(8,128)} %param.7, s32[]{:T(128)S(6)} %select_n.29, f32[]{:T(128)S(6)} %mul.257), kind=kOutput, calls=%fused_computation.10 | convolution fusion | flops 2718056448 | bytes 20054024 | tf_op jit(solution)/shard_map/dot_general | solution.py:27
  33.4 59.2 %all-reduce.11.cloned.1.call-done = f32[48,1536]{1,0:T(8,128)} async-done(((f32[48,1536]{1,0:T(8,128)}), f32[48,1536]{1,0:T(8,128)}) %all-reduce.11.cloned.1.call-update) | async-done | bytes 294928 | tf_op jit(solution)/shard_map/psum | solution.py:55
  92.7 1.0 fusion
  93.7 15.9 %convolution_subtract_fusion.4 = f32[48,3072]{1,0:T(8,128)} fusion(f32[1536,3072]{1,0:T(8,128)} %param.7, f32[48,3072]{1,0:T(8,128)S(1)} %fusion, f32[]{:T(128)S(6)} %mul.257, f32[48,1536]{1,0:T(8,128)} %all-reduce.11.cloned.1.call-done, f32[]{:T(128)S(6)} %mul.261, f32[]{:T(128)S(6)} %div.103), kind=kOutput, calls=%fused_computation.5 | convolution fusion | flops 2718351360 | bytes 20348940 | tf_op jit(solution)/shard_map/dot_general | solution.py:34
  109.6 0.6 all-reduce.15.cloned.1.call-start
  110.3 84.0 %all-reduce.13.cloned.1.call-done = f32[48,3072]{1,0:T(8,128)} async-done(((f32[48,3072]{1,0:T(8,128)}), f32[48,3072]{1,0:T(8,128)}) %all-reduce.13.cloned.1.call-update) | async-done | bytes 589840 | tf_op jit(solution)/shard_map/psum | solution.py:57
  194.3 1.1 multiply_subtract_fusion.3
  195.5 21.3 %convolution_subtract_fusion.8 = f32[48,1536]{1,0:T(8,128)} fusion(f32[48,3072]{1,0:T(8,128)S(1)} %multiply_subtract_fusion.3, f32[1536,3072]{1,0:T(8,128)} %param.7, s32[]{:T(128)S(6)} %select_n.29, f32[]{:T(128)S(6)} %mul.257), kind=kOutput, calls=%fused_computation.9 | convolution fusion | flops 2718056448 | bytes 20054024 | tf_op jit(solution)/shard_map/dot_general | solution.py:27
  216.9 58.7 %all-reduce.15.cloned.1.call-done = f32[48,1536]{1,0:T(8,128)} async-done(((f32[48,1536]{1,0:T(8,128)}), f32[48,1536]{1,0:T(8,128)}) %all-reduce.15.cloned.1.call-update) | async-done | bytes 294928 | tf_op jit(solution)/shard_map/psum | solution.py:55
  275.6 1.0 constant_dynamic-update-slice_fusion.2
  276.7 15.2 %convolution_subtract_fusion.3 = f32[48,3072]{1,0:T(8,128)} fusion(f32[48,1536]{1,0:T(8,128)S(1)} %get-tuple-element.12, f32[1536,3072]{1,0:T(8,128)} %param.7, f32[48,3072]{1,0:T(8,128)S(1)} %get-tuple-element.11, f32[]{:T(128)S(6)} %mul.257), kind=kOutput, calls=%fused_computation.4 | convolution fusion | flops 2718203904 | bytes 20348932 | tf_op jit(solution)/shard_map/dot_general | solution.py:34
  292.2 84.5 %all-reduce.17.cloned.1.call-done = f32[48,3072]{1,0:T(8,128)} async-done(((f32[48,3072]{1,0:T(8,128)}), f32[48,3072]{1,0:T(8,128)}) %all-reduce.17.cloned.1.call-update) | async-done | bytes 589840 | tf_op jit(solution)/shard_map/psum | solution.py:57
  376.7 1.1 multiply_subtract_fusion.2
  377.8 21.3 %convolution_subtract_fusion.7 = f32[48,1536]{1,0:T(8,128)} fusion(f32[48,3072]{1,0:T(8,128)S(1)} %multiply_subtract_fusion.2, f32[1536,3072]{1,0:T(8,128)} %param.7, s32[]{:T(128)S(6)} %select_n.29, f32[]{:T(128)S(6)} %mul.257), kind=kOutput, calls=%fused_computation.8 | convolution fusion | flops 2718056448 | bytes 20054024 | tf_op jit(solution)/shard_map/dot_general | solution.py:27
  399.2 58.7 %all-reduce.19.cloned.1.call-done = f32[48,1536]{1,0:T(8,128)} async-done(((f32[48,1536]{1,0:T(8,128)}), f32[48,1536]{1,0:T(8,128)}) %all-reduce.19.cloned.1.call-update) | async-done | bytes 294928 | tf_op jit(solution)/shard_map/psum | solution.py:55
  458.0 1.0 constant_dynamic-update-slice_fusion.1
  459.0 15.2 %convolution_subtract_fusion.2 = f32[48,3072]{1,0:T(8,128)} fusion(f32[48,1536]{1,0:T(8,128)S(1)} %get-tuple-element.10, f32[1536,3072]{1,0:T(8,128)} %param.7, f32[48,3072]{1,0:T(8,128)S(1)} %get-tuple-element.9, f32[]{:T(128)S(6)} %mul.257), kind=kOutput, calls=%fused_computation.3 | convolution fusion | flops 2718203904 | bytes 20348932 | tf_op jit(solution)/shard_map/dot_general | solution.py:34
  474.2 0.3 all-reduce.23.cloned.1.call-start
  474.6 84.4 %all-reduce.21.cloned.1.call-done = f32[48,3072]{1,0:T(8,128)} async-done(((f32[48,3072]{1,0:T(8,128)}), f32[48,3072]{1,0:T(8,128)}) %all-reduce.21.cloned.1.call-update) | async-done | bytes 589840 | tf_op jit(solution)/shard_map/psum | solution.py:57
  559.0 1.1 multiply_subtract_fusion.1
  560.1 21.3 %convolution_subtract_fusion.6 = f32[48,1536]{1,0:T(8,128)} fusion(f32[48,3072]{1,0:T(8,128)S(1)} %multiply_subtract_fusion.1, f32[1536,3072]{1,0:T(8,128)} %param.7, s32[]{:T(128)S(6)} %select_n.29, f32[]{:T(128)S(6)} %mul.257), kind=kOutput, calls=%fused_computation.7 | convolution fusion | flops 2718056448 | bytes 20054024 | tf_op jit(solution)/shard_map/dot_general | solution.py:27
  581.5 58.7 %all-reduce.23.cloned.1.call-done = f32[48,1536]{1,0:T(8,128)} async-done(((f32[48,1536]{1,0:T(8,128)}), f32[48,1536]{1,0:T(8,128)}) %all-reduce.23.cloned.1.call-update) | async-done | bytes 294928 | tf_op jit(solution)/shard_map/psum | solution.py:55
  640.3 1.0 constant_dynamic-update-slice_fusion
  641.3 15.2 %convolution_subtract_fusion.1 = f32[48,3072]{1,0:T(8,128)} fusion(f32[48,1536]{1,0:T(8,128)S(1)} %get-tuple-element.8, f32[1536,3072]{1,0:T(8,128)} %param.7, f32[48,3072]{1,0:T(8,128)S(1)} %get-tuple-element.6, f32[]{:T(128)S(6)} %mul.257), kind=kOutput, calls=%fused_computation.2 | convolution fusion | flops 2718203904 | bytes 20348932 | tf_op jit(solution)/shard_map/dot_general | solution.py:34
  656.5 0.3 all-reduce.27.cloned.1.call-start
  656.9 84.4 %all-reduce.25.cloned.1.call-done = f32[48,3072]{1,0:T(8,128)} async-done(((f32[48,3072]{1,0:T(8,128)}), f32[48,3072]{1,0:T(8,128)}) %all-reduce.25.cloned.1.call-update) | async-done | bytes 589840 | tf_op jit(solution)/shard_map/psum | solution.py:57
  741.3 1.1 multiply_subtract_fusion
  742.4 21.3 %convolution_subtract_fusion.5 = f32[48,1536]{1,0:T(8,128)} fusion(f32[48,3072]{1,0:T(8,128)S(1)} %multiply_subtract_fusion, f32[1536,3072]{1,0:T(8,128)} %param.7, s32[]{:T(128)S(6)} %select_n.29, f32[]{:T(128)S(6)} %mul.257), kind=kOutput, calls=%fused_computation.6 | convolution fusion | flops 2718056448 | bytes 20054024 | tf_op jit(solution)/shard_map/dot_general | solution.py:27
  763.8 58.7 %all-reduce.27.cloned.1.call-done = f32[48,1536]{1,0:T(8,128)} async-done(((f32[48,1536]{1,0:T(8,128)}), f32[48,1536]{1,0:T(8,128)}) %all-reduce.27.cloned.1.call-update) | async-done | bytes 294928 | tf_op jit(solution)/shard_map/psum | solution.py:55
  822.6 1.0 fusion.3
  823.6 15.9 %convolution_subtract_fusion = f32[48,3072]{1,0:T(8,128)} fusion(f32[1536,3072]{1,0:T(8,128)} %param.7, f32[48,3072]{1,0:T(8,128)S(1)} %fusion.3, f32[]{:T(128)S(6)} %mul.257, f32[48,1536]{1,0:T(8,128)S(1)} %get-tuple-element.8, f32[48,1536]{1,0:T(8,128)} %all-reduce.27.cloned.1.call-done, f32[]{:T(128)S(6)} %mul.309, f32[]{:T(128)S(6)} %div.109), kind=kOutput, calls=%fused_computation.1 | convolution fusion | flops 2718425088 | bytes 20643852 | tf_op jit(solution)/shard_map/dot_general | solution.py:34
  839.6 84.7 %all-reduce.29.cloned.1.call-done = f32[48,3072]{1,0:T(8,128)} async-done(((f32[48,3072]{1,0:T(8,128)}), f32[48,3072]{1,0:T(8,128)}) %all-reduce.29.cloned.1.call-update) | async-done | bytes 589840 | tf_op jit(solution)/shard_map/psum | solution.py:57
  924.3 1.2 subtract_select_fusion
  925.5 0.6 fusion.14
  926.1 23.4 %psum.94 = f32[48,48]{0,1:T(8,128)S(1)} all-reduce(f32[48,48]{0,1:T(8,128)S(1)} %fusion.14), channel_id=1, replica_groups=mesh['row'=16,'col'=8] {'col'}, use_global_device_ids=true, to_apply=%region_10.11 | all-reduce | flops 2304 | bytes 18432 | tf_op jit(solution)/shard_map/psum | solution.py:66
  949.6 4.4 cholesky.44
  954.0 0.6 compare_reduce_fusion.1
  954.6 0.7 fusion.4
  955.3 3.7 custom-call.6
  959.0 0.7 fusion.8
  959.7 0.6 fusion.15
  960.3 23.6 %psum.95 = f32[48,48]{0,1:T(8,128)S(1)} all-reduce(f32[48,48]{0,1:T(8,128)S(1)} %fusion.15), channel_id=1, replica_groups=mesh['row'=16,'col'=8] {'col'}, use_global_device_ids=true, to_apply=%region_13.16 | all-reduce | flops 2304 | bytes 18432 | tf_op jit(solution)/shard_map/psum | solution.py:66
  984.0 4.4 cholesky.55
  988.4 0.6 compare_reduce_fusion
  989.0 0.7 fusion.5
  989.7 3.7 custom-call.7
  993.4 1.5 convolution_multiply_fusion
  (35 shorter events, 1.0 us)
Async XLA Ops:
  6.5 86.1 %all-reduce.11.cloned.1.call-start = ((), (), s32[]{:S(2)}) async-start(), calls=%async_computation | async-start | bytes 589824 | tf_op jit(solution)/shard_map/psum | solution.py:55
  9.2 185.1 %copy-start.1 = (f32[48,3072]{1,0:T(8,128)S(1)}, f32[48,3072]{1,0:T(8,128)}, u32[]{:S(2)}) copy-start(f32[48,3072]{1,0:T(8,128)} %param.8) | copy-start | bytes 1769476
  31.3 163.0 %all-reduce.13.cloned.1.call-start = ((), (), s32[]{:S(2)}) async-start(), calls=%async_computation.1 | async-start | bytes 1179648 | tf_op jit(solution)/shard_map/psum | solution.py:57
  93.7 182.0 %copy-start = (f32[48,1536]{1,0:T(8,128)S(1)}, f32[48,1536]{1,0:T(8,128)}, u32[]{:S(2)}) copy-start(f32[48,1536]{1,0:T(8,128)} %all-reduce.11.cloned.1.call-done) | copy-start | bytes 884740
  109.6 166.0 %all-reduce.15.cloned.1.call-start = ((), (), s32[]{:S(2)}) async-start(), calls=%async_computation.2 | async-start | bytes 589824 | tf_op jit(solution)/shard_map/psum | solution.py:55
  216.7 159.9 %all-reduce.17.cloned.1.call-start = ((), (), s32[]{:S(2)}) async-start(), calls=%async_computation.3 | async-start | bytes 1179648 | tf_op jit(solution)/shard_map/psum | solution.py:57
  291.9 166.0 %all-reduce.19.cloned.1.call-start = ((), (), s32[]{:S(2)}) async-start(), calls=%async_computation.4 | async-start | bytes 589824 | tf_op jit(solution)/shard_map/psum | solution.py:55
  399.1 159.9 %all-reduce.21.cloned.1.call-start = ((), (), s32[]{:S(2)}) async-start(), calls=%async_computation.5 | async-start | bytes 1179648 | tf_op jit(solution)/shard_map/psum | solution.py:57
  474.2 166.0 %all-reduce.23.cloned.1.call-start = ((), (), s32[]{:S(2)}) async-start(), calls=%async_computation.6 | async-start | bytes 589824 | tf_op jit(solution)/shard_map/psum | solution.py:55
  581.4 159.9 %all-reduce.25.cloned.1.call-start = ((), (), s32[]{:S(2)}) async-start(), calls=%async_computation.7 | async-start | bytes 1179648 | tf_op jit(solution)/shard_map/psum | solution.py:57
  656.5 166.0 %all-reduce.27.cloned.1.call-start = ((), (), s32[]{:S(2)}) async-start(), calls=%async_computation.8 | async-start | bytes 589824 | tf_op jit(solution)/shard_map/psum | solution.py:55
  742.4 97.2 %copy-start.2 = (s32[48]{0:T(128)S(1)}, s32[48]{0:T(128)}, u32[]{:S(2)}) copy-start(s32[48]{0:T(128)} %param.10) | copy-start | bytes 580
  763.7 160.6 %all-reduce.29.cloned.1.call-start = ((), (), s32[]{:S(2)}) async-start(), calls=%async_computation.9 | async-start | bytes 1179648 | tf_op jit(solution)/shard_map/psum | solution.py:57
Sparse Core Ops, SparseCore 0:
  31.4 61.1 all-reduce.10
  109.7 84.5 all-reduce.12
  216.9 58.6 all-reduce.14
  292.0 84.6 all-reduce.16
  399.2 58.6 all-reduce.18
  474.4 84.5 all-reduce.20
  581.5 58.6 all-reduce.22
  656.6 84.5 all-reduce.24
  763.8 58.6 all-reduce.26
  839.6 84.6 all-reduce.28
where the time goes:
time: 1010 us; the launch traced here: 1000 us
  waiting for transfers between devices  716 us (71%)
  matrix products  188 us (19%)
  blocking collectives  47 us (5%)
  other arithmetic  29.6 us (3%)
  between operations  18.4 us (2%)
    psum x5, waiting for transfers between devices, on_device(): total = lax.psum(partial_value, 'row')  422 us
    psum x5, waiting for transfers between devices, on_device(): total = lax.psum(partial_value, 'col')  294 us
    dot_general x5, matrix products, toward_rows(): lax.dot_general(block, hamilton, (((1,), (1,)), ((), ())), precision=lax....  107 us
    dot_general x5, matrix products, toward_cols(): part_sum = jnp.dot(block, hamilton, precision=lax.Precision.HIGHEST)  77.4 us
    psum x2, blocking collectives, gram_of(): return lax.psum(local_gram, 'col')  47 us
  transfers between devices with their start and end apart: 10, of which 10 were waited for; matrix products, arithmetic and copies ran while one was open for 0% of the time, Pallas kernels for 0%

commit v1 on v0

v1 whole, which is shorter than its diff:
```python
import functools

import jax
import jax.numpy as jnp
from jax import lax
from jax.experimental import pallas as pl
from jax.experimental.pallas import tpu as pltpu
from jax.sharding import PartitionSpec as P

DLO = 6
DHI = 10
NEV = 48
LANES = 128
SUB = 8
TPB = NEV // SUB
MESH = pl.DeviceIdType.MESH
NT = (((1,), (1,)), ((), ()))
NN = (((1,), (0,)), ((), ()))
FAR_FIRST = (2, 1, 3, 0)
F32 = jnp.float32
BF16 = jnp.bfloat16


def split_planes(value):
    high = value.astype(BF16)
    low = (value - high.astype(F32)).astype(BF16)
    return high, low


def fold(product):
    return product[:NEV] + product[NEV:]


def kernel(
    sizes,
    ham_ref, start_ref, bounds_ref, pick_ref, out_ref,
    stage, high_ref, low_ref, planes, chunk_planes, filtered_ref,
    part_o, part_e, land_o, land_e, vec_o, vec_e, last_o, last_e, kept_ref,
    pick_tiles, gram_a, gram_b, work,
    ham_sem,
    rs_o_s, rs_o_r, ag_o_s, ag_o_r, rs_e_s, rs_e_r, ag_e_s, ag_e_r, g_s, g_r, h_s, h_r,
):
    rows_dev, cols_dev = sizes
    row = lax.axis_index("row")
    col = lax.axis_index("col")
    y, x = row // 4, lax.rem(row, 4)
    z, core = col // 2, lax.rem(col, 2)
    blocks_o, blocks_e = rows_dev // LANES, cols_dev // LANES
    own_o = blocks_o * TPB // 8
    own_e = blocks_e * TPB // 16
    grp_o = rows_dev // 4
    grp_e = cols_dev // 4

    peers_o = [(dz, dc) for dz in FAR_FIRST for dc in (0, 1) if (dz, dc) != (0, 0)]
    peers_e = [(dy, dx) for dy in FAR_FIRST for dx in FAR_FIRST if (dy, dx) != (0, 0)]

    def index_o(offset):
        return lax.rem(z + offset[0], 4) * 2 + lax.rem(core + offset[1], 2)

    def index_e(offset):
        return lax.rem(y + offset[0], 4) * 4 + lax.rem(x + offset[1], 4)

    def tiles_o(index):
        return pl.ds(index * own_o, own_o)

    def tiles_e(index):
        return pl.ds(index * own_e, own_e)

    def scatter_o(slot):
        to = index_o(peers_o[slot])
        return pltpu.make_async_remote_copy(
            src_ref=part_o.at[tiles_o(to)], dst_ref=land_o.at[slot],
            send_sem=rs_o_s.at[slot], recv_sem=rs_o_r.at[slot],
            device_id=(row, to), device_id_type=MESH)

    def scatter_e(slot):
        to = index_e(peers_e[slot])
        return pltpu.make_async_remote_copy(
            src_ref=part_e.at[tiles_e(to)], dst_ref=land_e.at[slot],
            send_sem=rs_e_s.at[slot], recv_sem=rs_e_r.at[slot],
            device_id=(to, col), device_id_type=MESH)

    def gather_o(slot):
        mine = vec_o.at[tiles_o(col)]
        return pltpu.make_async_remote_copy(
            src_ref=mine, dst_ref=mine,
            send_sem=ag_o_s.at[slot], recv_sem=ag_o_r.at[slot],
            device_id=(row, index_o(peers_o[slot])), device_id_type=MESH)

    def gather_e(slot):
        mine = vec_e.at[tiles_e(row)]
        return pltpu.make_async_remote_copy(
            src_ref=mine, dst_ref=mine,
            send_sem=ag_e_s.at[slot], recv_sem=ag_e_r.at[slot],
            device_id=(index_e(peers_e[slot]), col), device_id_type=MESH)

    def gram_copy(buffer, send, recv, slot):
        return pltpu.make_async_remote_copy(
            src_ref=buffer.at[col], dst_ref=buffer.at[col],
            send_sem=send.at[slot], recv_sem=recv.at[slot],
            device_id=(row, index_o(peers_o[slot])), device_id_type=MESH)

    def ham_copy(place):
        at = lax.rem(z + FAR_FIRST[place], 4) * grp_o
        return pltpu.make_async_copy(
            ham_ref.at[pl.ds(pl.multiple_of(at, LANES), grp_o)], stage.at[place], ham_sem.at[place])

    for place in range(4):
        ham_copy(place).start()

    barrier = pltpu.get_barrier_semaphore()
    for offset in peers_o:
        pl.semaphore_signal(barrier, inc=1, device_id=(row, index_o(offset)), device_id_type=MESH)
    for offset in peers_e:
        pl.semaphore_signal(barrier, inc=1, device_id=(index_e(offset), col), device_id_type=MESH)
    pl.semaphore_wait(barrier, len(peers_o) + len(peers_e))

    lowest = jnp.full((SUB, LANES), bounds_ref[0], F32)
    lower_end = jnp.full((SUB, LANES), bounds_ref[1], F32)
    upper_end = jnp.full((SUB, LANES), bounds_ref[2], F32)
    half_width = (upper_end - lower_end) / 2.0
    center = (upper_end + lower_end) / 2.0
    sigma_one = half_width / (lowest - center)

    vector_at = lax.broadcasted_iota(jnp.int32, (TPB, SUB, LANES), 0) * SUB + lax.broadcasted_iota(
        jnp.int32, (TPB, SUB, LANES), 1)
    picked = jnp.zeros((TPB, SUB, LANES), jnp.int32)
    for v in range(NEV):
        picked = jnp.where(vector_at == v, pick_ref[v], picked)
    pick_tiles[...] = picked
    gram_a[...] = jnp.zeros_like(gram_a)
    gram_b[...] = jnp.zeros_like(gram_b)

    for b in range(blocks_e):
        value = start_ref[:, b * LANES:(b + 1) * LANES]
        high, low = split_planes(value)
        planes[0:NEV, b * LANES:(b + 1) * LANES] = high
        planes[NEV:2 * NEV, b * LANES:(b + 1) * LANES] = low
        vec_e[b * TPB:(b + 1) * TPB] = value.reshape(TPB, SUB, LANES)
    last_e[...] = vec_e[tiles_e(row)]
    last_o[...] = jnp.zeros_like(last_o)

    offset = row * rows_dev - col * cols_dev
    inside = (offset >= 0) & (offset < cols_dev)
    diag_at = jnp.where(inside, offset, 0)
    diag_weight = jnp.where(inside, 1.0, 0.0).astype(F32)
    eye = (lax.broadcasted_iota(jnp.int32, (LANES, LANES), 0)
           == lax.broadcasted_iota(jnp.int32, (LANES, LANES), 1))
    shift = jnp.where(eye, center[0:1] * diag_weight, 0.0)

    def store_tiles(part, first_tile, total, blocks, add):
        for b in range(blocks):
            tile = total[:, b * LANES:(b + 1) * LANES].reshape(TPB, SUB, LANES)
            at = pl.ds(first_tile + b * TPB, TPB)
            if add:
                tile = tile + part[at]
            part[at] = tile

    def to_planes(vec, first_tile, blocks):
        for b in range(blocks):
            value = vec[pl.ds(first_tile + b * TPB, TPB)].reshape(NEV, LANES)
            high, low = split_planes(value)
            chunk_planes[0:NEV, b * LANES:(b + 1) * LANES] = high
            chunk_planes[NEV:2 * NEV, b * LANES:(b + 1) * LANES] = low

    def slots_o(dz):
        return [s for s, p in enumerate(peers_o) if p[0] == dz]

    def slots_e(dy):
        return [s for s, p in enumerate(peers_e) if p[0] == dy]

    for place, dz in enumerate(FAR_FIRST):
        group = lax.rem(z + dz, 4)
        ham_copy(place).wait()
        for b in range(grp_o // LANES):
            at = pl.ds(pl.multiple_of(diag_at + group * grp_o + b * LANES, LANES), LANES)
            rows_at = slice(b * LANES, (b + 1) * LANES)
            stage[place, rows_at, at] = stage[place, rows_at, at] - shift

        def split_rows(i, carry):
            from_row = pl.multiple_of(i * 16, 16)
            high, low = split_planes(stage[place, pl.ds(from_row, 16), :])
            to_row = pl.multiple_of(group * grp_o + i * 16, 16)
            high_ref[pl.ds(to_row, 16), :] = high
            low_ref[pl.ds(to_row, 16), :] = low
            return carry

        lax.fori_loop(0, grp_o // 16, split_rows, 0)
        rows_at = pl.ds(pl.multiple_of(group * grp_o, LANES), grp_o)
        total = fold(
            lax.dot_general(planes[...], high_ref[rows_at, :], NT, preferred_element_type=F32)
            + lax.dot_general(planes[...], low_ref[rows_at, :], NT, preferred_element_type=F32))
        store_tiles(part_o, group * (grp_o // LANES * TPB), total, grp_o // LANES, False)
        for slot in slots_o(dz):
            scatter_o(slot).start()

    def reduce_o(scale, coeff):
        for slot in range(len(peers_o)):
            scatter_o(slot).wait_recv()
        total = part_o[tiles_o(col)]
        for slot in range(len(peers_o)):
            total = total + land_o[slot]
        value = scale * total - coeff * last_o[...]
        last_o[...] = value
        vec_o[tiles_o(col)] = value
        for slot in range(len(peers_o)):
            gather_o(slot).start()
        for slot in range(len(peers_o)):
            scatter_o(slot).wait_send()

    def reduce_e(scale, coeff):
        for slot in range(len(peers_e)):
            scatter_e(slot).wait_recv()
        total = part_e[tiles_e(row)]
        for slot in range(len(peers_e)):
            total = total + land_e[slot]
        value = scale * total - coeff * last_e[...]
        last_e[...] = value
        return value

    def spread_e(value):
        vec_e[tiles_e(row)] = value
        for slot in range(len(peers_e)):
            gather_e(slot).start()
        for slot in range(len(peers_e)):
            scatter_e(slot).wait_send()

    def product_e():
        width = grp_o // LANES
        for turn, dz in enumerate(FAR_FIRST):
            for slot in slots_o(dz):
                gather_o(slot).wait_recv()
            group = lax.rem(z + 4 - dz, 4)
            to_planes(vec_o, group * (width * TPB), width)
            left = chunk_planes[:, 0:grp_o]
            rows_at = pl.ds(pl.multiple_of(group * grp_o, LANES), grp_o)
            for dy in FAR_FIRST:
                target = lax.rem(y + dy, 4)
                cols_at = pl.ds(pl.multiple_of(target * grp_e, LANES), grp_e)
                total = fold(
                    lax.dot_general(left, high_ref[rows_at, cols_at], NN, preferred_element_type=F32)
                    + lax.dot_general(left, low_ref[rows_at, cols_at], NN, preferred_element_type=F32))
                store_tiles(part_e, target * (grp_e // LANES * TPB), total, grp_e // LANES, turn > 0)
                if turn == 3:
                    for slot in slots_e(dy):
                        scatter_e(slot).start()
        for slot in range(len(peers_o)):
            gather_o(slot).wait_send()

    def product_o():
        width = grp_e // LANES
        for turn, dy in enumerate(FAR_FIRST):
            for slot in slots_e(dy):
                gather_e(slot).wait_recv()
            group = lax.rem(y + 4 - dy, 4)
            to_planes(vec_e, group * (width * TPB), width)
            left = chunk_planes[:, 0:grp_e]
            cols_at = pl.ds(pl.multiple_of(group * grp_e, LANES), grp_e)
            for dz in FAR_FIRST:
                target = lax.rem(z + dz, 4)
                rows_at = pl.ds(pl.multiple_of(target * grp_o, LANES), grp_o)
                total = fold(
                    lax.dot_general(left, high_ref[rows_at, cols_at], NT, preferred_element_type=F32)
                    + lax.dot_general(left, low_ref[rows_at, cols_at], NT, preferred_element_type=F32))
                store_tiles(part_o, target * (grp_o // LANES * TPB), total, grp_o // LANES, turn > 0)
                if turn == 3:
                    for slot in slots_o(dz):
                        scatter_o(slot).start()
        for slot in range(len(peers_e)):
            gather_e(slot).wait_send()

    def next_sigma(sigma):
        new_sigma = 1.0 / (2.0 / sigma_one - sigma)
        return 2.0 * new_sigma / half_width, sigma * new_sigma, new_sigma

    reduce_o(sigma_one / half_width, 0.0 * sigma_one)

    def two_steps(pair, sigma):
        scale, coeff, sigma = next_sigma(sigma)
        product_e()
        value = reduce_e(scale, coeff)
        kept_ref[...] = value * jnp.where(pair == DLO // 2 - 1, 1.0, 0.0) + jnp.where(
            pair == DLO // 2 - 1, jnp.zeros_like(value), kept_ref[...])
        spread_e(value)
        scale, coeff, sigma = next_sigma(sigma)
        product_o()
        reduce_o(scale, coeff)
        return sigma

    kept_ref[...] = jnp.zeros_like(kept_ref)
    sigma = lax.fori_loop(0, DHI // 2 - 1, two_steps, sigma_one)
    scale, coeff, sigma = next_sigma(sigma)
    product_e()
    value = reduce_e(scale, coeff)
    kept_ref[...] = jnp.where(
        jnp.stack([pick_tiles[lax.rem(row * own_e + t, TPB)] for t in range(own_e)]) == 0,
        kept_ref[...], value)
    spread_e(kept_ref[...])

    for dy in FAR_FIRST:
        for slot in slots_e(dy):
            gather_e(slot).wait_recv()
    for b in range(blocks_e):
        filtered_ref[:, b * LANES:(b + 1) * LANES] = vec_e[b * TPB:(b + 1) * TPB].reshape(NEV, LANES)
    for slot in range(len(peers_e)):
        gather_e(slot).wait_send()

    lane = lax.broadcasted_iota(jnp.int32, (NEV, LANES), 1)
    sublane = lax.broadcasted_iota(jnp.int32, (NEV, LANES), 0)

    def inverse_factor(buffer, send, recv):
        value = filtered_ref[...]
        gram = lax.dot_general(value, value, NT, precision=lax.Precision.HIGHEST, preferred_element_type=F32)
        buffer[col, :, 0:NEV] = gram
        for slot in range(len(peers_o)):
            gram_copy(buffer, send, recv, slot).start()
        for slot in range(len(peers_o)):
            gram_copy(buffer, send, recv, slot).wait()
        total = buffer[0]
        for i in range(1, 8):
            total = total + buffer[i]
        work[...] = jnp.where(lane < NEV, total, jnp.where(lane - NEV == sublane, 1.0, 0.0))

        def eliminate(j, carry):
            pivot_row = work[pl.ds(j, 1), :]
            pivot = jnp.sum(jnp.where(lane[0:1] == j, pivot_row, 0.0), axis=1, keepdims=True)
            column = jnp.sum(jnp.where(lane == j, work[...], 0.0), axis=1, keepdims=True)
            factor = jnp.where(sublane[:, 0:1] > j, column / pivot, 0.0)
            scaled = pivot_row * lax.rsqrt(pivot)
            updated = work[...] - factor * pivot_row
            work[...] = jnp.where(sublane == j, scaled, updated)
            return carry

        lax.fori_loop(0, NEV, eliminate, 0)
        return work[:, NEV:2 * NEV]

    first = jnp.dot(inverse_factor(gram_a, g_s, g_r), filtered_ref[...],
                    precision=lax.Precision.HIGHEST, preferred_element_type=F32)
    filtered_ref[...] = first
    order = jnp.sqrt(jnp.full((NEV, NEV), 8 * cols_dev, F32))
    out_ref[...] = jnp.dot(order * inverse_factor(gram_b, h_s, h_r), filtered_ref[...],
                           precision=lax.Precision.HIGHEST, preferred_element_type=F32)


def on_device(hamilton, start_block, bounds, degree_pick):
    rows_dev, cols_dev = hamilton.shape
    tiles_o = rows_dev // LANES * TPB
    tiles_e = cols_dev // LANES * TPB
    own_o, own_e = tiles_o // 8, tiles_e // 16
    vmem = pltpu.VMEM
    dma = pltpu.SemaphoreType.DMA
    return pl.pallas_call(
        functools.partial(kernel, (rows_dev, cols_dev)),
        out_shape=jax.ShapeDtypeStruct((NEV, cols_dev), F32),
        in_specs=[
            pl.BlockSpec(memory_space=pl.ANY),
            pl.BlockSpec(memory_space=pltpu.VMEM),
            pl.BlockSpec(memory_space=pltpu.SMEM),
            pl.BlockSpec(memory_space=pltpu.SMEM),
        ],
        out_specs=pl.BlockSpec(memory_space=pltpu.VMEM),
        scratch_shapes=[
            vmem((4, rows_dev // 4, cols_dev), F32),
            vmem((rows_dev, cols_dev), BF16),
            vmem((rows_dev, cols_dev), BF16),
            vmem((2 * NEV, cols_dev), BF16),
            vmem((2 * NEV, cols_dev // 4), BF16),
            vmem((NEV, cols_dev), F32),
            vmem((tiles_o, SUB, LANES), F32),
            vmem((tiles_e, SUB, LANES), F32),
            vmem((7, own_o, SUB, LANES), F32),
            vmem((15, own_e, SUB, LANES), F32),
            vmem((tiles_o, SUB, LANES), F32),
            vmem((tiles_e, SUB, LANES), F32),
            vmem((own_o, SUB, LANES), F32),
            vmem((own_e, SUB, LANES), F32),
            vmem((own_e, SUB, LANES), F32),
            vmem((TPB, SUB, LANES), jnp.int32),
            vmem((8, NEV, LANES), F32),
            vmem((8, NEV, LANES), F32),
            vmem((NEV, LANES), F32),
            dma((4,)),
            dma((7,)), dma((7,)), dma((7,)), dma((7,)),
            dma((15,)), dma((15,)), dma((15,)), dma((15,)),
            dma((7,)), dma((7,)), dma((7,)), dma((7,)),
        ],
        compiler_params=pltpu.CompilerParams(
            collective_id=0, has_side_effects=True, vmem_limit_bytes=56 * 2**20),
        cost_estimate=pl.CostEstimate(
            flops=2 * DHI * 4 * NEV * rows_dev * cols_dev,
            bytes_accessed=4 * rows_dev * cols_dev, transcendentals=0),
    )(hamilton, start_block, bounds, degree_pick)


def solution(mesh):
    in_specs = (P("row", "col"), P(None, "col"), P(), P())
    out_specs = P(None, "col")
    return jax.shard_map(
        on_device, mesh=mesh, in_specs=in_specs, out_specs=out_specs, check_vma=False
    )
```

time: 1010 us -> 216 us (0.21)
  waiting for transfers between devices: 716 us -> 0 us
  Pallas kernels: 0 us -> 214 us
  matrix products: 188 us -> 0 us
  blocking collectives: 47 us -> 0 us
  other arithmetic: 29.6 us -> 0 us
  between operations: 18.4 us -> 0.01 us
    psum x10 -> x0, waiting for transfers between devices: 716 us -> none  [the longest x5 422 us: on_device(): total = lax.psum(partial_value, 'row')]
    pallas_call x0 -> x1, Pallas kernels: none -> 214 us  [on_device(): pl.pallas_call(functools.partial(kernel, (rows_dev, cols_dev)), out_shape...]
    dot_general x12 -> x0, matrix products: 186 us -> none  [the longest x5 107 us: toward_rows(): lax.dot_general(block, hamilton, (((1,), (1,)), ((), ())), precision=lax....]
    psum x2 -> x0, blocking collectives: 47 us -> none  [gram_of(): return lax.psum(local_gram, 'col')]
    another operation x10 -> x0, other arithmetic: 18.8 us -> none  [the longest x6 10.1 us: cholesky_step(): lower_factor = jnp.linalg.cholesky(gram_of(block))]
  transfers between devices with their start and end apart: 10 -> 0, of which waited for: 10 -> 0; matrix products, arithmetic and copies ran while one was open for 0% -> 0% of each run, Pallas kernels for 0% -> 0%
where the time goes in v1:
time: 216 us
  Pallas kernels  214 us (99%)
    pallas_call x1, Pallas kernels, on_device(): pl.pallas_call(functools.partial(kernel, (rows_dev, cols_dev)), out_shape...  214 us

profile of v1, /device:TPU:1, one launch (start us, length us, event | category | flops | bytes accessed | tf_op | source)
XLA Modules:
  0.0 215.7 jit_solution(11774795028105608264)
XLA Ops:
  0.0 213.8 %shard_map.46 = f32[48,3072]{1,0:T(8,128)} custom-call(f32[1536,3072]{1,0:T(8,128)} %ham_ref.1, f32[48,3072]{1,0:T(8,128)} %start_ref.1, f32[3]{0:T(128)} %bounds_ref.1, s32[48]{0:T(128)} %pick_ref.1), custom_call_target="tpu_custom_call" | custom-call | flops 18119393280 | bytes 18874368 | tf_op jit(solution)/shard_map/pallas_call | solution.py:352
  213.8 1.9 copy.6

commit v2 on v1

v2 whole, which is shorter than its diff:
```python
import functools

import jax
import jax.numpy as jnp
from jax import lax
from jax.experimental import pallas as pl
from jax.experimental.pallas import tpu as pltpu
from jax.sharding import PartitionSpec as P

DLO = 6
DHI = 10
NEV = 48
GROUPS = 2
GV = NEV // GROUPS
PADV = 32
LANES = 128
SUB = 8
TPB = GV // SUB
PAIR = 9
FIVE = 5
FOUR = 4
CHUNK = 256
SLOTS = 4
MESH = pl.DeviceIdType.MESH
NT = (((1,), (1,)), ((), ()))
NN = (((1,), (0,)), ((), ()))
FAR_FIRST = (2, 1, 3, 0)
F32 = jnp.float32
BF16 = jnp.bfloat16


def split_planes(value):
    high = value.astype(BF16)
    low = (value - high.astype(F32)).astype(BF16)
    return high, low


def kernel(
    sizes,
    ham_ref, start_ref, bounds_ref, pick_ref, out_ref,
    stage, high_ref, low_ref, high_t, low_t, planes, group_planes, filtered_ref,
    part_o, part_e, land_o, land_e, vec_o, vec_e, last_o, last_e, kept_ref,
    pick_tiles, gram_a, gram_b, work,
    ham_sem,
    rs_o_s, rs_o_r, ag_o_s, ag_o_r, rs_e_s, rs_e_r, ag_e_s, ag_e_r,
    ax_o_s, ax_o_r, ax_e_s, ax_e_r, g_s, g_r, h_s, h_r,
):
    rows_dev, cols_dev = sizes
    row = lax.axis_index("row")
    col = lax.axis_index("col")
    y, x = row // 4, lax.rem(row, 4)
    z, core = col // 2, lax.rem(col, 2)
    blocks_o, blocks_e = rows_dev // LANES, cols_dev // LANES
    wide = cols_dev // 4
    wide_tiles = wide // LANES * TPB
    odd_row = lax.rem(row, 2)

    peers_o = [(dz, dc) for dz in FAR_FIRST for dc in (0, 1) if (dz, dc) != (0, 0)]
    peers_e = [(dy, dx) for dy in FAR_FIRST for dx in FAR_FIRST if (dy, dx) != (0, 0)]
    all_o, all_e = range(len(peers_o)), range(len(peers_e))

    def index_o(offset):
        return lax.rem(z + offset[0], 4) * 2 + lax.rem(core + offset[1], 2)

    def index_e(offset):
        return lax.rem(y + offset[0], 4) * 4 + lax.rem(x + offset[1], 4)

    def summed(index):
        return pl.ds((index // 2) * PAIR + lax.rem(index, 2) * FOUR, FIVE)

    def four(index):
        return pl.ds((index // 2) * PAIR + lax.rem(index, 2) * FIVE, FOUR)

    def fifth(index):
        return pl.ds((index // 2) * PAIR + FOUR, 1)

    def scatter_o(g, slot):
        to = index_o(peers_o[slot])
        return pltpu.make_async_remote_copy(
            src_ref=part_o.at[g, summed(to)], dst_ref=land_o.at[g, slot],
            send_sem=rs_o_s.at[g, slot], recv_sem=rs_o_r.at[g, slot],
            device_id=(row, to), device_id_type=MESH)

    def scatter_e(g, slot):
        to = index_e(peers_e[slot])
        return pltpu.make_async_remote_copy(
            src_ref=part_e.at[g, summed(to)], dst_ref=land_e.at[g, slot],
            send_sem=rs_e_s.at[g, slot], recv_sem=rs_e_r.at[g, slot],
            device_id=(to, col), device_id_type=MESH)

    def gather_o(g, slot, extra):
        mine = vec_o.at[g, fifth(col) if extra else four(col)]
        send, recv = (ax_o_s, ax_o_r) if extra else (ag_o_s, ag_o_r)
        return pltpu.make_async_remote_copy(
            src_ref=mine, dst_ref=mine, send_sem=send.at[g, slot], recv_sem=recv.at[g, slot],
            device_id=(row, index_o(peers_o[slot])), device_id_type=MESH)

    def gather_e(g, slot, extra):
        mine = vec_e.at[g, fifth(row) if extra else four(row)]
        send, recv = (ax_e_s, ax_e_r) if extra else (ag_e_s, ag_e_r)
        return pltpu.make_async_remote_copy(
            src_ref=mine, dst_ref=mine, send_sem=send.at[g, slot], recv_sem=recv.at[g, slot],
            device_id=(index_e(peers_e[slot]), col), device_id_type=MESH)

    def spread(vec, g, value, index, odd, gather, slots):
        @pl.when(odd == 0)
        def _():
            vec[g, pl.ds((index // 2) * PAIR, FIVE)] = value
            for slot in slots:
                gather(g, slot, False).start()
                gather(g, slot, True).start()

        @pl.when(odd == 1)
        def _():
            vec[g, pl.ds((index // 2) * PAIR + FIVE, FOUR)] = value[1:]
            for slot in slots:
                gather(g, slot, False).start()

    def arrived(g, odd, gather, peers):
        for slot in range(len(peers)):
            gather(g, slot, False).wait_recv()

        @pl.when(odd == 0)
        def _():
            for slot, offset in enumerate(peers):
                if offset[1] % 2 == 0:
                    gather(g, slot, True).wait_recv()

        @pl.when(odd == 1)
        def _():
            for slot, offset in enumerate(peers):
                if offset[1] % 2 == 1:
                    gather(g, slot, True).wait_recv()

    def left(g, odd, gather, slots):
        for slot in slots:
            gather(g, slot, False).wait_send()

        @pl.when(odd == 0)
        def _():
            for slot in slots:
                gather(g, slot, True).wait_send()

    def gram_copy(buffer, send, recv, slot):
        return pltpu.make_async_remote_copy(
            src_ref=buffer.at[col], dst_ref=buffer.at[col],
            send_sem=send.at[slot], recv_sem=recv.at[slot],
            device_id=(row, index_o(peers_o[slot])), device_id_type=MESH)

    chunks = rows_dev // CHUNK

    def chunk_at(place):
        half = lax.rem(z // 2 + 1 + place // (chunks // 2), 2)
        return pl.multiple_of(half * wide + place % (chunks // 2) * CHUNK, CHUNK)

    def ham_copy(place):
        return pltpu.make_async_copy(
            ham_ref.at[pl.ds(chunk_at(place), CHUNK)], stage.at[place % SLOTS], ham_sem.at[place % SLOTS])

    for place in range(SLOTS):
        ham_copy(place).start()

    barrier = pltpu.get_barrier_semaphore()
    for offset in peers_o:
        pl.semaphore_signal(barrier, inc=1, device_id=(row, index_o(offset)), device_id_type=MESH)
    for offset in peers_e:
        pl.semaphore_signal(barrier, inc=1, device_id=(index_e(offset), col), device_id_type=MESH)

    lowest = jnp.full((SUB, LANES), bounds_ref[0], F32)
    lower_end = jnp.full((SUB, LANES), bounds_ref[1], F32)
    upper_end = jnp.full((SUB, LANES), bounds_ref[2], F32)
    half_width = (upper_end - lower_end) / 2.0
    center = (upper_end + lower_end) / 2.0
    sigma_one = half_width / (lowest - center)

    tile_shape = (NEV // SUB, SUB, LANES)
    vector_at = lax.broadcasted_iota(jnp.int32, tile_shape, 0) * SUB + lax.broadcasted_iota(
        jnp.int32, tile_shape, 1)
    picked = jnp.zeros(tile_shape, jnp.int32)
    for v in range(NEV):
        picked = jnp.where(vector_at == v, pick_ref[v], picked)
    pick_tiles[...] = picked
    gram_a[...] = jnp.zeros_like(gram_a)
    gram_b[...] = jnp.zeros_like(gram_b)

    for b in range(blocks_e):
        value = start_ref[:, b * LANES:(b + 1) * LANES]
        high, low = split_planes(value)
        planes[0:NEV, b * LANES:(b + 1) * LANES] = high
        planes[NEV:2 * NEV, b * LANES:(b + 1) * LANES] = low
        for g in range(GROUPS):
            vec_e[g, b * TPB:(b + 1) * TPB] = value[g * GV:(g + 1) * GV].reshape(TPB, SUB, LANES)
    for g in range(GROUPS):
        last_e[g] = vec_e[g, summed(row)]
    last_o[...] = jnp.zeros_like(last_o)

    offset = row * rows_dev - col * cols_dev
    inside = (offset >= 0) & (offset < cols_dev)
    diag_at = jnp.where(inside, offset, 0)
    diag_weight = jnp.where(inside, 1.0, 0.0).astype(F32)
    eye = (lax.broadcasted_iota(jnp.int32, (LANES, LANES), 0)
           == lax.broadcasted_iota(jnp.int32, (LANES, LANES), 1))
    shift = jnp.where(eye, center[0:1] * diag_weight, 0.0)

    def store_tiles(part, g, first_tile, total):
        for b in range(total.shape[1] // LANES):
            part[g, pl.ds(first_tile + b * TPB, TPB)] = total[:, b * LANES:(b + 1) * LANES].reshape(
                TPB, SUB, LANES)

    for place in range(chunks):
        slot = place % SLOTS
        ham_copy(place).wait()
        first_row = chunk_at(place)
        for b in range(CHUNK // LANES):
            at = pl.ds(pl.multiple_of(diag_at + first_row + b * LANES, LANES), LANES)
            rows_at = slice(b * LANES, (b + 1) * LANES)
            stage[slot, rows_at, at] = stage[slot, rows_at, at] - shift

        def split_rows(i, carry):
            high, low = split_planes(stage[slot, pl.ds(pl.multiple_of(i * 16, 16), 16), :])
            to_row = pl.multiple_of(first_row + i * 16, 16)
            high_ref[pl.ds(to_row, 16), :] = high
            low_ref[pl.ds(to_row, 16), :] = low
            return carry

        lax.fori_loop(0, CHUNK // 16, split_rows, 0)
        if place + SLOTS < chunks:
            ham_copy(place + SLOTS).start()
        rows_at = pl.ds(first_row, CHUNK)
        total = (lax.dot_general(planes[...], high_ref[rows_at, :], NT, preferred_element_type=F32)
                 + lax.dot_general(planes[...], low_ref[rows_at, :], NT, preferred_element_type=F32))
        total = total[:NEV] + total[NEV:]
        for g in range(GROUPS):
            store_tiles(part_o, g, first_row // LANES * TPB, total[g * GV:(g + 1) * GV])
        if place == chunks // 2 - 1:
            pl.semaphore_wait(barrier, len(peers_o) + len(peers_e))

    def same_half(offset):
        return lax.rem(z + offset[0], 4) // 2 == z // 2

    for g in range(GROUPS):
        for slot in all_o:
            scatter_o(g, slot).start()

    def transpose(piece):
        rows_at = slice(piece * (rows_dev // 4), (piece + 1) * (rows_dev // 4))
        for j in range(0, cols_dev, 512):
            high_t[j:j + 512, rows_at] = high_ref[rows_at, j:j + 512].T
            low_t[j:j + 512, rows_at] = low_ref[rows_at, j:j + 512].T

    def reduce(g, scale, coeff, part, land, last, index, scatter, slots):
        for slot in slots:
            scatter(g, slot).wait_recv()
        total = part[g, summed(index)]
        for slot in slots:
            total = total + land[g, slot]
        value = scale * total - coeff * last[g]
        last[g] = value
        return value

    def reduce_o(g, scale, coeff):
        value = reduce(g, scale, coeff, part_o, land_o, last_o, col, scatter_o, all_o)
        spread(vec_o, g, value, col, core, gather_o, all_o)
        for slot in all_o:
            scatter_o(g, slot).wait_send()

    def reduce_e(g, scale, coeff):
        return reduce(g, scale, coeff, part_e, land_e, last_e, row, scatter_e, all_e)

    def spread_e(g, value):
        spread(vec_e, g, value, row, odd_row, gather_e, all_e)
        for slot in all_e:
            scatter_e(g, slot).wait_send()

    def to_planes(vec, g, blocks):
        nothing = jnp.zeros((PADV - GV, LANES), F32)
        for b in range(blocks):
            value = vec[g, b * TPB:(b + 1) * TPB].reshape(GV, LANES)
            high, low = split_planes(jnp.concatenate([value, nothing], axis=0))
            group_planes[0:PADV, b * LANES:(b + 1) * LANES] = high
            group_planes[PADV:2 * PADV, b * LANES:(b + 1) * LANES] = low

    def product(depth, high, low, target):
        cols_at = pl.ds(pl.multiple_of(target * wide, LANES), wide)
        vectors = group_planes[:, 0:depth]
        total = (lax.dot_general(vectors, high[:, cols_at], NN, preferred_element_type=F32)
                 + lax.dot_general(vectors, low[:, cols_at], NN, preferred_element_type=F32))
        return total[:GV] + total[PADV:PADV + GV]

    def product_e(g):
        arrived(g, core, gather_o, peers_o)
        to_planes(vec_o, g, blocks_o)
        for dy in FAR_FIRST:
            target = lax.rem(y + dy, 4)
            store_tiles(part_e, g, target * wide_tiles, product(rows_dev, high_ref, low_ref, target))
            for slot, offset in enumerate(peers_e):
                if offset[0] == dy:
                    scatter_e(g, slot).start()
        left(g, core, gather_o, all_o)

    def product_o(g):
        arrived(g, odd_row, gather_e, peers_e)
        to_planes(vec_e, g, blocks_e)
        for other in (1, 0):
            target = lax.rem(z // 2 + other, 2)
            store_tiles(part_o, g, target * wide_tiles, product(cols_dev, high_t, low_t, target))
            for slot, offset in enumerate(peers_o):
                @pl.when(same_half(offset) if other == 0 else jnp.logical_not(same_half(offset)))
                def _():
                    scatter_o(g, slot).start()
        left(g, odd_row, gather_e, all_e)

    def next_sigma(sigma):
        new_sigma = 1.0 / (2.0 / sigma_one - sigma)
        return 2.0 * new_sigma / half_width, sigma * new_sigma, new_sigma

    transpose(0)
    transpose(1)
    for g in range(GROUPS):
        reduce_o(g, sigma_one / half_width, 0.0 * sigma_one)
    transpose(2)
    transpose(3)

    def two_steps(pair, sigma):
        scale, coeff, sigma = next_sigma(sigma)
        for g in range(GROUPS):
            product_e(g)
        for g in range(GROUPS):
            value = reduce_e(g, scale, coeff)
            kept_ref[g] = jnp.where(pair == DLO // 2 - 1, value, kept_ref[g])
            spread_e(g, value)
        scale, coeff, sigma = next_sigma(sigma)
        for g in range(GROUPS):
            product_o(g)
        for g in range(GROUPS):
            reduce_o(g, scale, coeff)
        return sigma

    kept_ref[...] = jnp.zeros_like(kept_ref)
    sigma = lax.fori_loop(0, DHI // 2 - 1, two_steps, sigma_one)
    scale, coeff, sigma = next_sigma(sigma)
    for g in range(GROUPS):
        product_e(g)
    first_tile = (row // 2) * PAIR + odd_row * FOUR
    for g in range(GROUPS):
        value = reduce_e(g, scale, coeff)
        degrees = jnp.stack([pick_tiles[g * TPB + lax.rem(first_tile + t, TPB)] for t in range(FIVE)])
        spread_e(g, jnp.where(degrees == 0, kept_ref[g], value))

    for g in range(GROUPS):
        arrived(g, odd_row, gather_e, peers_e)
        for b in range(blocks_e):
            filtered_ref[g * GV:(g + 1) * GV, b * LANES:(b + 1) * LANES] = vec_e[
                g, b * TPB:(b + 1) * TPB].reshape(GV, LANES)
    for g in range(GROUPS):
        left(g, odd_row, gather_e, all_e)

    lane = lax.broadcasted_iota(jnp.int32, (NEV, LANES), 1)
    sublane = lax.broadcasted_iota(jnp.int32, (NEV, LANES), 0)

    def inverse_factor(buffer, send, recv):
        high, low = split_planes(filtered_ref[...])
        planes[0:NEV] = high
        planes[NEV:2 * NEV] = low
        gram = lax.dot_general(planes[...], planes[...], NT, preferred_element_type=F32)
        gram = gram[:NEV] + gram[NEV:]
        buffer[col, :, 0:NEV] = gram[:, :NEV] + gram[:, NEV:]
        for slot in all_o:
            gram_copy(buffer, send, recv, slot).start()
        for slot in all_o:
            gram_copy(buffer, send, recv, slot).wait()
        total = buffer[0]
        for i in range(1, 8):
            total = total + buffer[i]
        work[...] = jnp.where(lane < NEV, total, jnp.where(lane - NEV == sublane, 1.0, 0.0))

        def eliminate(i, carry):
            j = 2 * i
            rest = work[...]
            row_a, row_b = work[pl.ds(j, 1), :], work[pl.ds(j + 1, 1), :]
            at_a, at_b = lane == j, lane == j + 1

            def entry(mask, values):
                return jnp.sum(jnp.where(mask, values, 0.0), axis=1, keepdims=True)

            pivot_a = entry(at_a[0:1], row_a)
            cross = entry(at_b[0:1], row_a) / pivot_a
            pivot_b = entry(at_b[0:1], row_b) - cross * entry(at_b[0:1], row_a)
            column_a, column_b = entry(at_a, rest), entry(at_b, rest)
            row_b = row_b - cross * row_a
            below = sublane[:, 0:1] > j + 1
            factor_a = jnp.where(below, column_a / pivot_a, 0.0)
            factor_b = jnp.where(below, (column_b - cross * column_a) / pivot_b, 0.0)
            updated = rest - factor_a * row_a - factor_b * row_b
            work[...] = jnp.where(sublane == j, row_a * lax.rsqrt(pivot_a), jnp.where(
                sublane == j + 1, row_b * lax.rsqrt(pivot_b), updated))
            return carry

        lax.fori_loop(0, NEV // 2, eliminate, 0)
        return work[:, NEV:2 * NEV]

    first = jnp.dot(inverse_factor(gram_a, g_s, g_r), filtered_ref[...],
                    precision=lax.Precision.HIGHEST, preferred_element_type=F32)
    filtered_ref[...] = first
    order = jnp.sqrt(jnp.full((NEV, NEV), 8 * cols_dev, F32))
    out_ref[...] = jnp.dot(order * inverse_factor(gram_b, h_s, h_r), filtered_ref[...],
                           precision=lax.Precision.HIGHEST, preferred_element_type=F32)


def on_device(hamilton, start_block, bounds, degree_pick):
    rows_dev, cols_dev = hamilton.shape
    tiles_o = rows_dev // LANES * TPB
    tiles_e = cols_dev // LANES * TPB
    vmem = pltpu.VMEM
    dma = pltpu.SemaphoreType.DMA
    return pl.pallas_call(
        functools.partial(kernel, (rows_dev, cols_dev)),
        out_shape=jax.ShapeDtypeStruct((NEV, cols_dev), F32),
        in_specs=[
            pl.BlockSpec(memory_space=pl.ANY),
            pl.BlockSpec(memory_space=pltpu.VMEM),
            pl.BlockSpec(memory_space=pltpu.SMEM),
            pl.BlockSpec(memory_space=pltpu.SMEM),
        ],
        out_specs=pl.BlockSpec(memory_space=pltpu.VMEM),
        scratch_shapes=[
            vmem((SLOTS, CHUNK, cols_dev), F32),
            vmem((rows_dev, cols_dev), BF16),
            vmem((rows_dev, cols_dev), BF16),
            vmem((cols_dev, rows_dev), BF16),
            vmem((cols_dev, rows_dev), BF16),
            vmem((2 * NEV, cols_dev), BF16),
            vmem((2 * PADV, cols_dev), BF16),
            vmem((NEV, cols_dev), F32),
            vmem((GROUPS, tiles_o, SUB, LANES), F32),
            vmem((GROUPS, tiles_e, SUB, LANES), F32),
            vmem((GROUPS, 7, FIVE, SUB, LANES), F32),
            vmem((GROUPS, 15, FIVE, SUB, LANES), F32),
            vmem((GROUPS, tiles_o, SUB, LANES), F32),
            vmem((GROUPS, tiles_e, SUB, LANES), F32),
            vmem((GROUPS, FIVE, SUB, LANES), F32),
            vmem((GROUPS, FIVE, SUB, LANES), F32),
            vmem((GROUPS, FIVE, SUB, LANES), F32),
            vmem((NEV // SUB, SUB, LANES), jnp.int32),
            vmem((8, NEV, LANES), F32),
            vmem((8, NEV, LANES), F32),
            vmem((NEV, LANES), F32),
            dma((SLOTS,)),
            dma((GROUPS, 7)), dma((GROUPS, 7)), dma((GROUPS, 7)), dma((GROUPS, 7)),
            dma((GROUPS, 15)), dma((GROUPS, 15)), dma((GROUPS, 15)), dma((GROUPS, 15)),
            dma((GROUPS, 7)), dma((GROUPS, 7)), dma((GROUPS, 15)), dma((GROUPS, 15)),
            dma((7,)), dma((7,)), dma((7,)), dma((7,)),
        ],
        compiler_params=pltpu.CompilerParams(
            collective_id=0, has_side_effects=True, vmem_limit_bytes=62 * 2**20),
        cost_estimate=pl.CostEstimate(
            flops=2 * DHI * 4 * NEV * rows_dev * cols_dev,
            bytes_accessed=4 * rows_dev * cols_dev, transcendentals=0),
    )(hamilton, start_block, bounds, degree_pick)


def solution(mesh):
    in_specs = (P("row", "col"), P(None, "col"), P(), P())
    out_specs = P(None, "col")
    return jax.shard_map(
        on_device, mesh=mesh, in_specs=in_specs, out_specs=out_specs, check_vma=False
    )
```

time: 216 us -> 188 us (0.87)
  Pallas kernels: 214 us -> 186 us
    pallas_call x1, Pallas kernels: 214 us -> 186 us  [on_device(): pl.pallas_call(functools.partial(kernel, (rows_dev, cols_dev)), out_shape...]
where the time goes in v2:
time: 188 us
  Pallas kernels  186 us (99%)
  local copies, waits for them, and re-layouts  1.92 us (1%)
    pallas_call x1, Pallas kernels, on_device(): pl.pallas_call(functools.partial(kernel, (rows_dev, cols_dev)), out_shape...  186 us

profile of v2, /device:TPU:1, one launch (start us, length us, event | category | flops | bytes accessed | tf_op | source)
XLA Modules:
  0.0 187.9 jit_solution(12007378442493511155)
XLA Ops:
  0.0 185.9 %shard_map.46 = f32[48,3072]{1,0:T(8,128)} custom-call(f32[1536,3072]{1,0:T(8,128)} %ham_ref.1, f32[48,3072]{1,0:T(8,128)} %start_ref.1, f32[3]{0:T(128)} %bounds_ref.1, s32[48]{0:T(128)} %pick_ref.1), custom_call_target="tpu_custom_call" | custom-call | flops 18119393280 | bytes 18874368 | tf_op jit(solution)/shard_map/pallas_call | solution.py:416
  185.9 1.9 %copy.6 = f32[48,3072]{1,0:T(8,128)} copy(f32[48,3072]{1,0:T(8,128)} %shard_map.46) | data formatting | bytes 1179648

commit v3 on v2

--- a/solution.py
+++ b/solution.py
@@ -37,13 +37,13 @@
 
 def kernel(
     sizes,
-    ham_ref, start_ref, bounds_ref, pick_ref, out_ref,
-    stage, high_ref, low_ref, high_t, low_t, planes, group_planes, filtered_ref,
+    ham_ref, start_hbm, bounds_ref, pick_ref, out_ref,
+    stage, high_ref, low_ref, high_t, low_t, planes, group_planes, start_ref,
     part_o, part_e, land_o, land_e, vec_o, vec_e, last_o, last_e, kept_ref,
     pick_tiles, gram_a, gram_b, work,
-    ham_sem,
+    ham_sem, start_sem,
     rs_o_s, rs_o_r, ag_o_s, ag_o_r, rs_e_s, rs_e_r, ag_e_s, ag_e_r,
-    ax_o_s, ax_o_r, ax_e_s, ax_e_r, g_s, g_r, h_s, h_r,
+    g_s, g_r, h_s, h_r,
 ):
     rows_dev, cols_dev = sizes
     row = lax.axis_index("row")
@@ -65,81 +65,89 @@
     def index_e(offset):
         return lax.rem(y + offset[0], 4) * 4 + lax.rem(x + offset[1], 4)
 
+    def shared(index, parity):
+        if parity == 0:
+            return pl.ds((index // 2) * PAIR, FIVE)
+        return pl.ds((index // 2) * PAIR + FIVE, FOUR)
+
+    def by_parity(odd, act):
+        for parity in (0, 1):
+            pl.when(odd == parity)(functools.partial(act, parity))
+
+    def landing(land, g, slot, parity):
+        return land.at[g, slot] if parity == 0 else land.at[g, slot, pl.ds(1, FOUR)]
+
+    def remote(source, target, send, recv, device):
+        return pltpu.make_async_remote_copy(
+            src_ref=source, dst_ref=target, send_sem=send, recv_sem=recv,
+            device_id=device, device_id_type=MESH)
+
+    def scatter_o(g, slot, parity):
+        to = index_o(peers_o[slot])
+        return remote(part_o.at[g, shared(to, parity)], landing(land_o, g, slot, parity),
+                      rs_o_s.at[g, slot], rs_o_r.at[g, slot], (row, to))
+
+    def scatter_e(g, slot, parity):
+        to = index_e(peers_e[slot])
+        return remote(part_e.at[g, shared(to, parity)], landing(land_e, g, slot, parity),
+                      rs_e_s.at[g, slot], rs_e_r.at[g, slot], (to, col))
+
+    def gather_o(g, slot, parity):
+        mine = vec_o.at[g, shared(col, parity)]
+        return remote(mine, mine, ag_o_s.at[g, slot], ag_o_r.at[g, slot], (row, index_o(peers_o[slot])))
+
+    def gather_e(g, slot, parity):
+        mine = vec_e.at[g, shared(row, parity)]
+        return remote(mine, mine, ag_e_s.at[g, slot], ag_e_r.at[g, slot], (index_e(peers_e[slot]), col))
+
+    def partner(parity, offset):
+        return (parity + offset[1]) % 2
+
+    def spread(vec, g, value, index, odd, gather, slots):
+        def act(parity):
+            vec[g, shared(index, parity)] = value[parity:]
+            for slot in slots:
+                gather(g, slot, parity).start()
+
+        by_parity(odd, act)
+
+    def arrived(g, odd, gather, peers):
+        def act(parity):
+            for slot, offset in enumerate(peers):
+                gather(g, slot, partner(parity, offset)).wait_recv()
+
+        by_parity(odd, act)
+
+    def left(g, odd, gather, slots):
+        def act(parity):
+            for slot in slots:
+                gather(g, slot, parity).wait_send()
+
+        by_parity(odd, act)
+
+    def send_parts(g, odd, scatter, peers, slots):
+        def act(parity):
+            for slot in slots:
+                scatter(g, slot, partner(parity, peers[slot])).start()
+
+        by_parity(odd, act)
+
+    def sent_parts(g, odd, scatter, peers):
+        def act(parity):
+            for slot, offset in enumerate(peers):
+                scatter(g, slot, partner(parity, offset)).wait_send()
+
+        by_parity(odd, act)
+
+    def parts_here(g, odd, scatter, slots):
+        def act(parity):
+            for slot in slots:
+                scatter(g, slot, parity).wait_recv()
+
+        by_parity(odd, act)
+
     def summed(index):
         return pl.ds((index // 2) * PAIR + lax.rem(index, 2) * FOUR, FIVE)
-
-    def four(index):
-        return pl.ds((index // 2) * PAIR + lax.rem(index, 2) * FIVE, FOUR)
-
-    def fifth(index):
-        return pl.ds((index // 2) * PAIR + FOUR, 1)
-
-    def scatter_o(g, slot):
-        to = index_o(peers_o[slot])
-        return pltpu.make_async_remote_copy(
-            src_ref=part_o.at[g, summed(to)], dst_ref=land_o.at[g, slot],
-            send_sem=rs_o_s.at[g, slot], recv_sem=rs_o_r.at[g, slot],
-            device_id=(row, to), device_id_type=MESH)
-
-    def scatter_e(g, slot):
-        to = index_e(peers_e[slot])
-        return pltpu.make_async_remote_copy(
-            src_ref=part_e.at[g, summed(to)], dst_ref=land_e.at[g, slot],
-            send_sem=rs_e_s.at[g, slot], recv_sem=rs_e_r.at[g, slot],
-            device_id=(to, col), device_id_type=MESH)
-
-    def gather_o(g, slot, extra):
-        mine = vec_o.at[g, fifth(col) if extra else four(col)]
-        send, recv = (ax_o_s, ax_o_r) if extra else (ag_o_s, ag_o_r)
-        return pltpu.make_async_remote_copy(
-            src_ref=mine, dst_ref=mine, send_sem=send.at[g, slot], recv_sem=recv.at[g, slot],
-            device_id=(row, index_o(peers_o[slot])), device_id_type=MESH)
-
-    def gather_e(g, slot, extra):
-        mine = vec_e.at[g, fifth(row) if extra else four(row)]
-        send, recv = (ax_e_s, ax_e_r) if extra else (ag_e_s, ag_e_r)
-        return pltpu.make_async_remote_copy(
-            src_ref=mine, dst_ref=mine, send_sem=send.at[g, slot], recv_sem=recv.at[g, slot],
-            device_id=(index_e(peers_e[slot]), col), device_id_type=MESH)
-
-    def spread(vec, g, value, index, odd, gather, slots):
-        @pl.when(odd == 0)
-        def _():
-            vec[g, pl.ds((index // 2) * PAIR, FIVE)] = value
-            for slot in slots:
-                gather(g, slot, False).start()
-                gather(g, slot, True).start()
-
-        @pl.when(odd == 1)
-        def _():
-            vec[g, pl.ds((index // 2) * PAIR + FIVE, FOUR)] = value[1:]
-            for slot in slots:
-                gather(g, slot, False).start()
-
-    def arrived(g, odd, gather, peers):
-        for slot in range(len(peers)):
-            gather(g, slot, False).wait_recv()
-
-        @pl.when(odd == 0)
-        def _():
-            for slot, offset in enumerate(peers):
-                if offset[1] % 2 == 0:
-                    gather(g, slot, True).wait_recv()
-
-        @pl.when(odd == 1)
-        def _():
-            for slot, offset in enumerate(peers):
-                if offset[1] % 2 == 1:
-                    gather(g, slot, True).wait_recv()
-
-    def left(g, odd, gather, slots):
-        for slot in slots:
-            gather(g, slot, False).wait_send()
-
-        @pl.when(odd == 0)
-        def _():
-            for slot in slots:
-                gather(g, slot, True).wait_send()
 
     def gram_copy(buffer, send, recv, slot):
         return pltpu.make_async_remote_copy(
@@ -149,17 +157,22 @@
 
     chunks = rows_dev // CHUNK
 
-    def chunk_at(place):
-        half = lax.rem(z // 2 + 1 + place // (chunks // 2), 2)
-        return pl.multiple_of(half * wide + place % (chunks // 2) * CHUNK, CHUNK)
-
     def ham_copy(place):
         return pltpu.make_async_copy(
-            ham_ref.at[pl.ds(chunk_at(place), CHUNK)], stage.at[place % SLOTS], ham_sem.at[place % SLOTS])
-
+            ham_ref.at[place * CHUNK:(place + 1) * CHUNK], stage.at[place % SLOTS], ham_sem.at[place % SLOTS])
+
+    start_copy = pltpu.make_async_copy(start_hbm, start_ref, start_sem)
+    start_copy.start()
     for place in range(SLOTS):
         ham_copy(place).start()
 
+    for g in range(GROUPS):
+        for slot in all_o:
+            land_o[g, slot, 0] = jnp.zeros((SUB, LANES), F32)
+        for slot in all_e:
+            land_e[g, slot, 0] = jnp.zeros((SUB, LANES), F32)
+    gram_a[...] = jnp.zeros_like(gram_a)
+    gram_b[...] = jnp.zeros_like(gram_b)
     barrier = pltpu.get_barrier_semaphore()
     for offset in peers_o:
         pl.semaphore_signal(barrier, inc=1, device_id=(row, index_o(offset)), device_id_type=MESH)
@@ -180,9 +193,8 @@
     for v in range(NEV):
         picked = jnp.where(vector_at == v, pick_ref[v], picked)
     pick_tiles[...] = picked
-    gram_a[...] = jnp.zeros_like(gram_a)
-    gram_b[...] = jnp.zeros_like(gram_b)
-
+
+    start_copy.wait()
     for b in range(blocks_e):
         value = start_ref[:, b * LANES:(b + 1) * LANES]
         high, low = split_planes(value)
@@ -207,40 +219,46 @@
             part[g, pl.ds(first_tile + b * TPB, TPB)] = total[:, b * LANES:(b + 1) * LANES].reshape(
                 TPB, SUB, LANES)
 
-    for place in range(chunks):
-        slot = place % SLOTS
+    def split_chunk(place):
+        slot, first_row = place % SLOTS, place * CHUNK
         ham_copy(place).wait()
-        first_row = chunk_at(place)
         for b in range(CHUNK // LANES):
             at = pl.ds(pl.multiple_of(diag_at + first_row + b * LANES, LANES), LANES)
             rows_at = slice(b * LANES, (b + 1) * LANES)
             stage[slot, rows_at, at] = stage[slot, rows_at, at] - shift
-
-        def split_rows(i, carry):
-            high, low = split_planes(stage[slot, pl.ds(pl.multiple_of(i * 16, 16), 16), :])
-            to_row = pl.multiple_of(first_row + i * 16, 16)
-            high_ref[pl.ds(to_row, 16), :] = high
-            low_ref[pl.ds(to_row, 16), :] = low
-            return carry
-
-        lax.fori_loop(0, CHUNK // 16, split_rows, 0)
-        if place + SLOTS < chunks:
-            ham_copy(place + SLOTS).start()
-        rows_at = pl.ds(first_row, CHUNK)
+        for i in range(0, CHUNK, 16):
+            high, low = split_planes(stage[slot, i:i + 16, :])
+            high_ref[first_row + i:first_row + i + 16, :] = high
+            low_ref[first_row + i:first_row + i + 16, :] = low
+
+    def multiply_chunk(place):
+        rows_at = slice(place * CHUNK, (place + 1) * CHUNK)
         total = (lax.dot_general(planes[...], high_ref[rows_at, :], NT, preferred_element_type=F32)
                  + lax.dot_general(planes[...], low_ref[rows_at, :], NT, preferred_element_type=F32))
         total = total[:NEV] + total[NEV:]
         for g in range(GROUPS):
-            store_tiles(part_o, g, first_row // LANES * TPB, total[g * GV:(g + 1) * GV])
+            store_tiles(part_o, g, place * CHUNK // LANES * TPB, total[g * GV:(g + 1) * GV])
+
+    def in_half(offset, half):
+        return lax.rem(z + offset[0], 4) // 2 == half
+
+    def send_half(half):
+        for g in range(GROUPS):
+            for slot, offset in enumerate(peers_o):
+                pl.when(in_half(offset, half))(
+                    functools.partial(send_parts, g, core, scatter_o, peers_o, (slot,)))
+
+    split_chunk(0)
+    for place in range(chunks):
+        if place + SLOTS < chunks:
+            ham_copy(place + SLOTS).start()
+        if place + 1 < chunks:
+            split_chunk(place + 1)
+        multiply_chunk(place)
         if place == chunks // 2 - 1:
             pl.semaphore_wait(barrier, len(peers_o) + len(peers_e))
-
-    def same_half(offset):
-        return lax.rem(z + offset[0], 4) // 2 == z // 2
-
-    for g in range(GROUPS):
-        for slot in all_o:
-            scatter_o(g, slot).start()
+            send_half(0)
+    send_half(1)
 
     def transpose(piece):
         rows_at = slice(piece * (rows_dev // 4), (piece + 1) * (rows_dev // 4))
@@ -248,9 +266,8 @@
             high_t[j:j + 512, rows_at] = high_ref[rows_at, j:j + 512].T
             low_t[j:j + 512, rows_at] = low_ref[rows_at, j:j + 512].T
 
-    def reduce(g, scale, coeff, part, land, last, index, scatter, slots):
-        for slot in slots:
-            scatter(g, slot).wait_recv()
+    def reduce(g, scale, coeff, part, land, last, index, odd, scatter, slots):
+        parts_here(g, odd, scatter, slots)
         total = part[g, summed(index)]
         for slot in slots:
             total = total + land[g, slot]
@@ -259,18 +276,16 @@
         return value
 
     def reduce_o(g, scale, coeff):
-        value = reduce(g, scale, coeff, part_o, land_o, last_o, col, scatter_o, all_o)
+        value = reduce(g, scale, coeff, part_o, land_o, last_o, col, core, scatter_o, all_o)
         spread(vec_o, g, value, col, core, gather_o, all_o)
-        for slot in all_o:
-            scatter_o(g, slot).wait_send()
+        sent_parts(g, core, scatter_o, peers_o)
 
     def reduce_e(g, scale, coeff):
-        return reduce(g, scale, coeff, part_e, land_e, last_e, row, scatter_e, all_e)
+        return reduce(g, scale, coeff, part_e, land_e, last_e, row, odd_row, scatter_e, all_e)
 
     def spread_e(g, value):
         spread(vec_e, g, value, row, odd_row, gather_e, all_e)
-        for slot in all_e:
-            scatter_e(g, slot).wait_send()
+        sent_parts(g, odd_row, scatter_e, peers_e)
 
     def to_planes(vec, g, blocks):
         nothing = jnp.zeros((PADV - GV, LANES), F32)
@@ -293,9 +308,7 @@
         for dy in FAR_FIRST:
             target = lax.rem(y + dy, 4)
             store_tiles(part_e, g, target * wide_tiles, product(rows_dev, high_ref, low_ref, target))
-            for slot, offset in enumerate(peers_e):
-                if offset[0] == dy:
-                    scatter_e(g, slot).start()
+            send_parts(g, odd_row, scatter_e, peers_e, [s for s in all_e if peers_e[s][0] == dy])
         left(g, core, gather_o, all_o)
 
     def product_o(g):
@@ -305,9 +318,8 @@
             target = lax.rem(z // 2 + other, 2)
             store_tiles(part_o, g, target * wide_tiles, product(cols_dev, high_t, low_t, target))
             for slot, offset in enumerate(peers_o):
-                @pl.when(same_half(offset) if other == 0 else jnp.logical_not(same_half(offset)))
-                def _():
-                    scatter_o(g, slot).start()
+                pl.when(in_half(offset, target))(
+                    functools.partial(send_parts, g, core, scatter_o, peers_o, (slot,)))
         left(g, odd_row, gather_e, all_e)
 
     def next_sigma(sigma):
@@ -350,21 +362,24 @@
     for g in range(GROUPS):
         arrived(g, odd_row, gather_e, peers_e)
         for b in range(blocks_e):
-            filtered_ref[g * GV:(g + 1) * GV, b * LANES:(b + 1) * LANES] = vec_e[
-                g, b * TPB:(b + 1) * TPB].reshape(GV, LANES)
+            cols_at = slice(b * LANES, (b + 1) * LANES)
+            start_ref[g * GV:(g + 1) * GV, cols_at] = vec_e[g, b * TPB:(b + 1) * TPB].reshape(GV, LANES)
     for g in range(GROUPS):
         left(g, odd_row, gather_e, all_e)
 
     lane = lax.broadcasted_iota(jnp.int32, (NEV, LANES), 1)
     sublane = lax.broadcasted_iota(jnp.int32, (NEV, LANES), 0)
 
+    high, low = split_planes(start_ref[...])
+    planes[0:NEV] = high
+    planes[NEV:2 * NEV] = low
+
     def inverse_factor(buffer, send, recv):
-        high, low = split_planes(filtered_ref[...])
-        planes[0:NEV] = high
-        planes[NEV:2 * NEV] = low
         gram = lax.dot_general(planes[...], planes[...], NT, preferred_element_type=F32)
         gram = gram[:NEV] + gram[NEV:]
-        buffer[col, :, 0:NEV] = gram[:, :NEV] + gram[:, NEV:]
+        gram = gram[:, :NEV] + gram[:, NEV:]
+        buffer[col, :, 0:NEV] = gram[:GV]
+        buffer[col, :, LANES // 2:LANES // 2 + NEV] = gram[GV:]
         for slot in all_o:
             gram_copy(buffer, send, recv, slot).start()
         for slot in all_o:
@@ -372,6 +387,7 @@
         total = buffer[0]
         for i in range(1, 8):
             total = total + buffer[i]
+        total = jnp.concatenate([total, pltpu.roll(total, LANES // 2, 1)], axis=0)
         work[...] = jnp.where(lane < NEV, total, jnp.where(lane - NEV == sublane, 1.0, 0.0))
 
         def eliminate(i, carry):
@@ -399,12 +415,21 @@
         lax.fori_loop(0, NEV // 2, eliminate, 0)
         return work[:, NEV:2 * NEV]
 
-    first = jnp.dot(inverse_factor(gram_a, g_s, g_r), filtered_ref[...],
-                    precision=lax.Precision.HIGHEST, preferred_element_type=F32)
-    filtered_ref[...] = first
-    order = jnp.sqrt(jnp.full((NEV, NEV), 8 * cols_dev, F32))
-    out_ref[...] = jnp.dot(order * inverse_factor(gram_b, h_s, h_r), filtered_ref[...],
-                           precision=lax.Precision.HIGHEST, preferred_element_type=F32)
+    def apply_factor(factor, cols_at):
+        high, low = split_planes(factor)
+        factor_planes = jnp.concatenate([high, low], axis=0)
+        total = (jnp.dot(factor_planes, planes[0:NEV, cols_at], preferred_element_type=F32)
+                 + jnp.dot(factor_planes, planes[NEV:2 * NEV, cols_at], preferred_element_type=F32))
+        return total[:NEV] + total[NEV:]
+
+    factor = inverse_factor(gram_a, g_s, g_r)
+    for j in range(0, cols_dev, wide):
+        high, low = split_planes(apply_factor(factor, slice(j, j + wide)))
+        planes[0:NEV, j:j + wide] = high
+        planes[NEV:2 * NEV, j:j + wide] = low
+    factor = jnp.sqrt(jnp.full((NEV, NEV), 8 * cols_dev, F32)) * inverse_factor(gram_b, h_s, h_r)
+    for j in range(0, cols_dev, wide):
+        out_ref[:, j:j + wide] = apply_factor(factor, slice(j, j + wide))
 
 
 def on_device(hamilton, start_block, bounds, degree_pick):
@@ -418,7 +443,7 @@
         out_shape=jax.ShapeDtypeStruct((NEV, cols_dev), F32),
         in_specs=[
             pl.BlockSpec(memory_space=pl.ANY),
-            pl.BlockSpec(memory_space=pltpu.VMEM),
+            pl.BlockSpec(memory_space=pl.ANY),
             pl.BlockSpec(memory_space=pltpu.SMEM),
             pl.BlockSpec(memory_space=pltpu.SMEM),
         ],
@@ -442,13 +467,13 @@
             vmem((GROUPS, FIVE, SUB, LANES), F32),
             vmem((GROUPS, FIVE, SUB, LANES), F32),
             vmem((NEV // SUB, SUB, LANES), jnp.int32),
-            vmem((8, NEV, LANES), F32),
-            vmem((8, NEV, LANES), F32),
+            vmem((8, GV, LANES), F32),
+            vmem((8, GV, LANES), F32),
             vmem((NEV, LANES), F32),
             dma((SLOTS,)),
+            dma,
             dma((GROUPS, 7)), dma((GROUPS, 7)), dma((GROUPS, 7)), dma((GROUPS, 7)),
             dma((GROUPS, 15)), dma((GROUPS, 15)), dma((GROUPS, 15)), dma((GROUPS, 15)),
-            dma((GROUPS, 7)), dma((GROUPS, 7)), dma((GROUPS, 15)), dma((GROUPS, 15)),
             dma((7,)), dma((7,)), dma((7,)), dma((7,)),
         ],
         compiler_params=pltpu.CompilerParams(

time: 188 us -> 182 us (0.968)
  Pallas kernels: 186 us -> 180 us
    pallas_call x1, Pallas kernels: 186 us -> 180 us  [on_device(): pl.pallas_call(functools.partial(kernel, (rows_dev, cols_dev)), out_shape...]
where the time goes in v3:
time: 182 us
  Pallas kernels  180 us (99%)
  local copies, waits for them, and re-layouts  1.92 us (1%)
    pallas_call x1, Pallas kernels, on_device(): pl.pallas_call(functools.partial(kernel, (rows_dev, cols_dev)), out_shape...  180 us

profile of v3, /device:TPU:1, one launch (start us, length us, event | category | flops | bytes accessed | tf_op | source)
XLA Modules:
  0.0 182.3 jit_solution(13189346930226149312)
XLA Ops:
  0.0 180.4 %shard_map.46 = f32[48,3072]{1,0:T(8,128)} custom-call(f32[1536,3072]{1,0:T(8,128)} %ham_ref.1, f32[48,3072]{1,0:T(8,128)} %start_hbm.1, f32[3]{0:T(128)} %bounds_ref.1, s32[48]{0:T(128)} %pick_ref.1), custom_call_target="tpu_custom_call" | custom-call | flops 18119393280 | bytes 18874368 | tf_op jit(solution)/shard_map/pallas_call | solution.py:441
  180.4 1.9 %copy.6 = f32[48,3072]{1,0:T(8,128)} copy(f32[48,3072]{1,0:T(8,128)} %shard_map.46) | data formatting | bytes 1179648

commit v4 on v3

--- a/solution.py
+++ b/solution.py
@@ -77,6 +77,9 @@
     def landing(land, g, slot, parity):
         return land.at[g, slot] if parity == 0 else land.at[g, slot, pl.ds(1, FOUR)]
 
+    def landing_all(land, g, parity):
+        return land.at[g] if parity == 0 else land.at[g, :, pl.ds(1, FOUR)]
+
     def remote(source, target, send, recv, device):
         return pltpu.make_async_remote_copy(
             src_ref=source, dst_ref=target, send_sem=send, recv_sem=recv,
@@ -85,20 +88,20 @@
     def scatter_o(g, slot, parity):
         to = index_o(peers_o[slot])
         return remote(part_o.at[g, shared(to, parity)], landing(land_o, g, slot, parity),
-                      rs_o_s.at[g, slot], rs_o_r.at[g, slot], (row, to))
+                      rs_o_s.at[g], rs_o_r.at[g], (row, to))
 
     def scatter_e(g, slot, parity):
         to = index_e(peers_e[slot])
         return remote(part_e.at[g, shared(to, parity)], landing(land_e, g, slot, parity),
-                      rs_e_s.at[g, slot], rs_e_r.at[g, slot], (to, col))
+                      rs_e_s.at[g], rs_e_r.at[g], (to, col))
 
     def gather_o(g, slot, parity):
         mine = vec_o.at[g, shared(col, parity)]
-        return remote(mine, mine, ag_o_s.at[g, slot], ag_o_r.at[g, slot], (row, index_o(peers_o[slot])))
+        return remote(mine, mine, ag_o_s.at[g], ag_o_r.at[g], (row, index_o(peers_o[slot])))
 
     def gather_e(g, slot, parity):
         mine = vec_e.at[g, shared(row, parity)]
-        return remote(mine, mine, ag_e_s.at[g, slot], ag_e_r.at[g, slot], (index_e(peers_e[slot]), col))
+        return remote(mine, mine, ag_e_s.at[g], ag_e_r.at[g], (index_e(peers_e[slot]), col))
 
     def partner(parity, offset):
         return (parity + offset[1]) % 2
@@ -111,17 +114,20 @@
 
         by_parity(odd, act)
 
-    def arrived(g, odd, gather, peers):
-        def act(parity):
-            for slot, offset in enumerate(peers):
-                gather(g, slot, partner(parity, offset)).wait_recv()
-
-        by_parity(odd, act)
-
-    def left(g, odd, gather, slots):
-        def act(parity):
-            for slot in slots:
-                gather(g, slot, parity).wait_send()
+    def everything(buffer, g, parity):
+        return buffer.at[g, pl.ds(0, buffer.shape[1] - FIVE + parity)]
+
+    def arrived(g, odd, vec, recv):
+        def act(parity):
+            whole = everything(vec, g, parity)
+            remote(whole, whole, recv.at[g], recv.at[g], (row, index_o(peers_o[0]))).wait_recv()
+
+        by_parity(odd, act)
+
+    def left(g, odd, land, send):
+        def act(parity):
+            whole = landing_all(land, g, parity)
+            remote(whole, whole, send.at[g], send.at[g], (row, index_o(peers_o[0]))).wait_send()
 
         by_parity(odd, act)
 
@@ -132,17 +138,17 @@
 
         by_parity(odd, act)
 
-    def sent_parts(g, odd, scatter, peers):
-        def act(parity):
-            for slot, offset in enumerate(peers):
-                scatter(g, slot, partner(parity, offset)).wait_send()
-
-        by_parity(odd, act)
-
-    def parts_here(g, odd, scatter, slots):
-        def act(parity):
-            for slot in slots:
-                scatter(g, slot, parity).wait_recv()
+    def sent_parts(g, odd, part, send):
+        def act(parity):
+            whole = everything(part, g, parity)
+            remote(whole, whole, send.at[g], send.at[g], (row, index_o(peers_o[0]))).wait_send()
+
+        by_parity(odd, act)
+
+    def parts_here(g, odd, land, recv):
+        def act(parity):
+            whole = landing_all(land, g, parity)
+            remote(whole, whole, recv.at[g], recv.at[g], (row, index_o(peers_o[0]))).wait_recv()
 
         by_parity(odd, act)
 
@@ -266,8 +272,8 @@
             high_t[j:j + 512, rows_at] = high_ref[rows_at, j:j + 512].T
             low_t[j:j + 512, rows_at] = low_ref[rows_at, j:j + 512].T
 
-    def reduce(g, scale, coeff, part, land, last, index, odd, scatter, slots):
-        parts_here(g, odd, scatter, slots)
+    def reduce(g, scale, coeff, part, land, last, index, odd, recv, slots):
+        parts_here(g, odd, land, recv)
         total = part[g, summed(index)]
         for slot in slots:
             total = total + land[g, slot]
@@ -276,16 +282,16 @@
         return value
 
     def reduce_o(g, scale, coeff):
-        value = reduce(g, scale, coeff, part_o, land_o, last_o, col, core, scatter_o, all_o)
+        value = reduce(g, scale, coeff, part_o, land_o, last_o, col, core, rs_o_r, all_o)
         spread(vec_o, g, value, col, core, gather_o, all_o)
-        sent_parts(g, core, scatter_o, peers_o)
+        sent_parts(g, core, part_o, rs_o_s)
 
     def reduce_e(g, scale, coeff):
-        return reduce(g, scale, coeff, part_e, land_e, last_e, row, odd_row, scatter_e, all_e)
+        return reduce(g, scale, coeff, part_e, land_e, last_e, row, odd_row, rs_e_r, all_e)
 
     def spread_e(g, value):
         spread(vec_e, g, value, row, odd_row, gather_e, all_e)
-        sent_parts(g, odd_row, scatter_e, peers_e)
+        sent_parts(g, odd_row, part_e, rs_e_s)
 
     def to_planes(vec, g, blocks):
         nothing = jnp.zeros((PADV - GV, LANES), F32)
@@ -303,16 +309,16 @@
         return total[:GV] + total[PADV:PADV + GV]
 
     def product_e(g):
-        arrived(g, core, gather_o, peers_o)
+        arrived(g, core, vec_o, ag_o_r)
         to_planes(vec_o, g, blocks_o)
         for dy in FAR_FIRST:
             target = lax.rem(y + dy, 4)
             store_tiles(part_e, g, target * wide_tiles, product(rows_dev, high_ref, low_ref, target))
             send_parts(g, odd_row, scatter_e, peers_e, [s for s in all_e if peers_e[s][0] == dy])
-        left(g, core, gather_o, all_o)
+        left(g, core, land_o, ag_o_s)
 
     def product_o(g):
-        arrived(g, odd_row, gather_e, peers_e)
+        arrived(g, odd_row, vec_e, ag_e_r)
         to_planes(vec_e, g, blocks_e)
         for other in (1, 0):
             target = lax.rem(z // 2 + other, 2)
@@ -320,7 +326,7 @@
             for slot, offset in enumerate(peers_o):
                 pl.when(in_half(offset, target))(
                     functools.partial(send_parts, g, core, scatter_o, peers_o, (slot,)))
-        left(g, odd_row, gather_e, all_e)
+        left(g, odd_row, land_e, ag_e_s)
 
     def next_sigma(sigma):
         new_sigma = 1.0 / (2.0 / sigma_one - sigma)
@@ -360,12 +366,12 @@
         spread_e(g, jnp.where(degrees == 0, kept_ref[g], value))
 
     for g in range(GROUPS):
-        arrived(g, odd_row, gather_e, peers_e)
+        arrived(g, odd_row, vec_e, ag_e_r)
         for b in range(blocks_e):
             cols_at = slice(b * LANES, (b + 1) * LANES)
             start_ref[g * GV:(g + 1) * GV, cols_at] = vec_e[g, b * TPB:(b + 1) * TPB].reshape(GV, LANES)
     for g in range(GROUPS):
-        left(g, odd_row, gather_e, all_e)
+        left(g, odd_row, land_e, ag_e_s)
 
     lane = lax.broadcasted_iota(jnp.int32, (NEV, LANES), 1)
     sublane = lax.broadcasted_iota(jnp.int32, (NEV, LANES), 0)
@@ -472,8 +478,8 @@
             vmem((NEV, LANES), F32),
             dma((SLOTS,)),
             dma,
-            dma((GROUPS, 7)), dma((GROUPS, 7)), dma((GROUPS, 7)), dma((GROUPS, 7)),
-            dma((GROUPS, 15)), dma((GROUPS, 15)), dma((GROUPS, 15)), dma((GROUPS, 15)),
+            dma((GROUPS,)), dma((GROUPS,)), dma((GROUPS,)), dma((GROUPS,)),
+            dma((GROUPS,)), dma((GROUPS,)), dma((GROUPS,)), dma((GROUPS,)),
             dma((7,)), dma((7,)), dma((7,)), dma((7,)),
         ],
         compiler_params=pltpu.CompilerParams(

time: 182 us -> 181 us (level)
  Pallas kernels: 180 us -> 178 us
    pallas_call x1, Pallas kernels: 180 us -> 178 us  [on_device(): pl.pallas_call(functools.partial(kernel, (rows_dev, cols_dev)), out_shape...]
where the time goes in v4:
time: 181 us; the launch traced here: 180 us
  Pallas kernels  178 us (98%)
  local copies, waits for them, and re-layouts  1.92 us (1%)
    pallas_call x1, Pallas kernels, on_device(): pl.pallas_call(functools.partial(kernel, (rows_dev, cols_dev)), out_shape...  178 us

profile of v4, /device:TPU:1, one launch (start us, length us, event | category | flops | bytes accessed | tf_op | source)
XLA Modules:
  0.0 180.4 jit_solution(15280564596754486596)
XLA Ops:
  0.0 178.5 %shard_map.46 = f32[48,3072]{1,0:T(8,128)} custom-call(f32[1536,3072]{1,0:T(8,128)} %ham_ref.1, f32[48,3072]{1,0:T(8,128)} %start_hbm.1, f32[3]{0:T(128)} %bounds_ref.1, s32[48]{0:T(128)} %pick_ref.1), custom_call_target="tpu_custom_call" | custom-call | flops 18119393280 | bytes 18874368 | tf_op jit(solution)/shard_map/pallas_call | solution.py:447
  178.5 1.9 %copy.6 = f32[48,3072]{1,0:T(8,128)} copy(f32[48,3072]{1,0:T(8,128)} %shard_map.46) | data formatting | bytes 1179648

commit v5 on v4

--- a/solution.py
+++ b/solution.py
@@ -158,7 +158,7 @@
     def gram_copy(buffer, send, recv, slot):
         return pltpu.make_async_remote_copy(
             src_ref=buffer.at[col], dst_ref=buffer.at[col],
-            send_sem=send.at[slot], recv_sem=recv.at[slot],
+            send_sem=send, recv_sem=recv,
             device_id=(row, index_o(peers_o[slot])), device_id_type=MESH)
 
     chunks = rows_dev // CHUNK
@@ -388,8 +388,8 @@
         buffer[col, :, LANES // 2:LANES // 2 + NEV] = gram[GV:]
         for slot in all_o:
             gram_copy(buffer, send, recv, slot).start()
-        for slot in all_o:
-            gram_copy(buffer, send, recv, slot).wait()
+        others = buffer.at[pl.ds(0, len(peers_o))]
+        remote(others, others, send, recv, (row, index_o(peers_o[0]))).wait()
         total = buffer[0]
         for i in range(1, 8):
             total = total + buffer[i]
@@ -433,7 +433,7 @@
         high, low = split_planes(apply_factor(factor, slice(j, j + wide)))
         planes[0:NEV, j:j + wide] = high
         planes[NEV:2 * NEV, j:j + wide] = low
-    factor = jnp.sqrt(jnp.full((NEV, NEV), 8 * cols_dev, F32)) * inverse_factor(gram_b, h_s, h_r)
+    factor = inverse_factor(gram_b, h_s, h_r)
     for j in range(0, cols_dev, wide):
         out_ref[:, j:j + wide] = apply_factor(factor, slice(j, j + wide))
 
@@ -444,7 +444,7 @@
     tiles_e = cols_dev // LANES * TPB
     vmem = pltpu.VMEM
     dma = pltpu.SemaphoreType.DMA
-    return pl.pallas_call(
+    second = pl.pallas_call(
         functools.partial(kernel, (rows_dev, cols_dev)),
         out_shape=jax.ShapeDtypeStruct((NEV, cols_dev), F32),
         in_specs=[
@@ -480,7 +480,7 @@
             dma,
             dma((GROUPS,)), dma((GROUPS,)), dma((GROUPS,)), dma((GROUPS,)),
             dma((GROUPS,)), dma((GROUPS,)), dma((GROUPS,)), dma((GROUPS,)),
-            dma((7,)), dma((7,)), dma((7,)), dma((7,)),
+            dma, dma, dma, dma,
         ],
         compiler_params=pltpu.CompilerParams(
             collective_id=0, has_side_effects=True, vmem_limit_bytes=62 * 2**20),
@@ -488,6 +488,7 @@
             flops=2 * DHI * 4 * NEV * rows_dev * cols_dev,
             bytes_accessed=4 * rows_dev * cols_dev, transcendentals=0),
     )(hamilton, start_block, bounds, degree_pick)
+    return second * jnp.sqrt(jnp.float32(cols_dev * lax.axis_size("col")))
 
 
 def solution(mesh):

time: 181 us -> 180 us (level)
  other arithmetic: 0 us -> 1.93 us
  local copies, waits for them, and re-layouts: 1.92 us -> 0 us
    mul x0 -> x1, other arithmetic: none -> 1.93 us  [on_device(): return second * jnp.sqrt(jnp.float32(cols_dev * lax.axis_size('col')))]
    unnamed x1 -> x0, local copies, waits for them, and re-layouts: 1.92 us -> none
where the time goes in v5:
time: 180 us
  Pallas kernels  178 us (99%)
  other arithmetic  1.93 us (1%)
    pallas_call x1, Pallas kernels, on_device(): pl.pallas_call(functools.partial(kernel, (rows_dev, cols_dev)), out_shape...  178 us

profile of v5, /device:TPU:1, one launch (start us, length us, event | category | flops | bytes accessed | tf_op | source)
XLA Modules:
  0.0 180.2 jit_solution(12962667473973271896)
XLA Ops:
  0.0 178.2 %shard_map.46 = f32[48,3072]{1,0:T(8,128)} custom-call(f32[1536,3072]{1,0:T(8,128)} %ham_ref.1, f32[48,3072]{1,0:T(8,128)} %start_hbm.1, f32[3]{0:T(128)} %bounds_ref.1, s32[48]{0:T(128)} %pick_ref.1), custom_call_target="tpu_custom_call" | custom-call | flops 18119393280 | bytes 18874368 | tf_op jit(solution)/shard_map/pallas_call | solution.py:447
  178.2 1.9 %broadcast_multiply_fusion = f32[48,3072]{1,0:T(8,128)} fusion(f32[48,3072]{1,0:T(8,128)} %shard_map.46), kind=kLoop, calls=%fused_computation | loop fusion | flops 147456 | bytes 1179648 | tf_op jit(solution)/shard_map/mul | solution.py:491

commit v6 on v5

--- a/solution.py
+++ b/solution.py
@@ -248,11 +248,14 @@
     def in_half(offset, half):
         return lax.rem(z + offset[0], 4) // 2 == half
 
+    def slots_at(dz):
+        return [slot for slot in all_o if peers_o[slot][0] == dz]
+
     def send_half(half):
         for g in range(GROUPS):
-            for slot, offset in enumerate(peers_o):
-                pl.when(in_half(offset, half))(
-                    functools.partial(send_parts, g, core, scatter_o, peers_o, (slot,)))
+            for dz in FAR_FIRST:
+                pl.when(in_half((dz, 0), half))(
+                    functools.partial(send_parts, g, core, scatter_o, peers_o, slots_at(dz)))
 
     split_chunk(0)
     for place in range(chunks):
@@ -323,9 +326,9 @@
         for other in (1, 0):
             target = lax.rem(z // 2 + other, 2)
             store_tiles(part_o, g, target * wide_tiles, product(cols_dev, high_t, low_t, target))
-            for slot, offset in enumerate(peers_o):
-                pl.when(in_half(offset, target))(
-                    functools.partial(send_parts, g, core, scatter_o, peers_o, (slot,)))
+            for dz in FAR_FIRST:
+                pl.when(in_half((dz, 0), target))(
+                    functools.partial(send_parts, g, core, scatter_o, peers_o, slots_at(dz)))
         left(g, odd_row, land_e, ag_e_s)
 
     def next_sigma(sigma):

time: 180 us -> 180 us (level)
  no operation moved by 1% of the time
where the time goes in v6:
time: 180 us
  Pallas kernels  178 us (99%)
  other arithmetic  1.93 us (1%)
    pallas_call x1, Pallas kernels, on_device(): pl.pallas_call(functools.partial(kernel, (rows_dev, cols_dev)), out_shape...  178 us

profile of v6, /device:TPU:1, one launch (start us, length us, event | category | flops | bytes accessed | tf_op | source)
XLA Modules:
  0.0 180.2 jit_solution(4582157772649991260)
XLA Ops:
  0.0 178.2 %shard_map.46 = f32[48,3072]{1,0:T(8,128)} custom-call(f32[1536,3072]{1,0:T(8,128)} %ham_ref.1, f32[48,3072]{1,0:T(8,128)} %start_hbm.1, f32[3]{0:T(128)} %bounds_ref.1, s32[48]{0:T(128)} %pick_ref.1), custom_call_target="tpu_custom_call" | custom-call | flops 18119393280 | bytes 18874368 | tf_op jit(solution)/shard_map/pallas_call | solution.py:450
  178.3 1.9 %broadcast_multiply_fusion = f32[48,3072]{1,0:T(8,128)} fusion(f32[48,3072]{1,0:T(8,128)} %shard_map.46), kind=kLoop, calls=%fused_computation | loop fusion | flops 147456 | bytes 1179648 | tf_op jit(solution)/shard_map/mul | solution.py:494
